TPU v7x, 32 devices: a whole 2x2x4 slice. The times are simulated.
32 devices in a mesh: tile: 8 (over y, x, core), depth: 4 (over z).
Axes of the slice: x: 2, y: 2, z: 4, core: 2. Of those that a mesh axis runs over, the one named last changes fastest.
Arguments:
- estimate: float32 [8, 256, 1024], P('depth', 'tile'), may hold values from 0.25 to 4
- views: bfloat16 [8, 8, 256, 1024], P(None, 'depth', 'tile'), may hold values from 0.19921875 to 5
- kernel_x: float32 [8, 31], replicated, may hold values from 0.01 to 1
- kernel_y: float32 [8, 31], replicated, may hold values from 0.01 to 1
- kernel_z: float32 [8, 31], replicated, may hold values from 0.01 to 1
- offsets: int32 [8], replicated, may hold values from 16 to 96
Outputs:
- updated: float32 [8, 256, 1024], P('depth', 'tile')
All inputs are finite; a program needn't handle non-finite values.
Results may differ from a plain program's by a relative error of at most 0.0007.
Values may be sent and summed in bfloat16 or wider, within the bound.
No kernel may reach another device: no remote copies, remote signals or barrier semaphores. Data moves between devices by JAX's collectives and lax.ppermute only.
A program may use at most 128 MiB of HBM per device.

v0:
```python
import jax
import jax.numpy as jnp
from jax import lax
from jax.sharding import PartitionSpec as P


def extended(array, sides, width):
    for axis, dim in sides:
        devices, length = (lax.axis_size(axis), array.shape[dim])
        up = [(i, (i + 1) % devices) for i in range(devices - 1)]
        down = [(j, i) for i, j in up]
        last = lax.slice_in_dim(array, length - width, length, axis=dim)
        initial = lax.slice_in_dim(array, 0, width, axis=dim)
        before = lax.ppermute(last, axis, up)
        after = lax.ppermute(initial, axis, down)
        array = jnp.concatenate([before, array, after], axis=dim)
    return array


def normalize(kernel):
    return kernel / jnp.sum(kernel, axis=1, keepdims=True)


def tap_factor(kernel, tap_index, ndims):
    return kernel[:, tap_index].reshape((kernel.shape[0],) + (1,) * (ndims - 1))


def convolve(values, kernel, axis):
    margin = kernel.shape[1] // 2
    length = values.shape[axis]
    widths = [(0, 0)] * values.ndim
    widths[axis] = (margin, margin)
    padded = jnp.pad(values, widths)
    summed = jnp.zeros_like(values)
    for tap_index in range(kernel.shape[1]):
        summed = summed + tap_factor(kernel, tap_index, values.ndim) * lax.slice_in_dim(
            padded, tap_index, tap_index + length, axis=axis
        )
    return summed


def strip_pass(widened, kernel, length, axis):
    shape = list(widened.shape)
    shape[0] = kernel.shape[0]
    shape[axis] = length
    summed = jnp.zeros(tuple(shape), jnp.float32)
    for tap_index in range(kernel.shape[1]):
        summed = summed + tap_factor(kernel, tap_index, widened.ndim) * lax.slice_in_dim(
            widened, tap_index, tap_index + length, axis=axis
        )
    return summed


def shards(estimate, views, kernel_x, kernel_y, kernel_z, offsets):
    kernel_x = normalize(kernel_x)
    kernel_y = normalize(kernel_y)
    kernel_z = normalize(kernel_z)
    flipped_x = kernel_x[:, ::-1]
    flipped_y = kernel_y[:, ::-1]
    flipped_z = kernel_z[:, ::-1]
    margin = kernel_x.shape[1] // 2
    strip_rows = estimate.shape[1]
    slab_rows = strip_rows * lax.axis_size("tile")
    view_rows = 5 * slab_rows // 8
    tile_index = lax.axis_index("tile")
    row_ids = tile_index * strip_rows + jnp.arange(strip_rows, dtype=jnp.int32)
    inside = (row_ids[None, :] >= offsets[:, None]) & (
        row_ids[None, :] < offsets[:, None] + view_rows
    )
    covered = inside.astype(jnp.float32)
    coverage = jnp.sum(covered, axis=0)
    widened = extended(estimate.astype(jnp.bfloat16), (("tile", 1),), margin).astype(estimate.dtype)
    partial_blur = strip_pass(widened[None], kernel_x, strip_rows, 2)
    partial_blur = convolve(partial_blur, kernel_y, 3)
    deepened = lax.all_to_all(
        partial_blur.astype(jnp.bfloat16), "depth", split_axis=2, concat_axis=1, tiled=True
    ).astype(partial_blur.dtype)
    blurred_deep = convolve(deepened, kernel_z, 1)
    blurred = lax.all_to_all(
        blurred_deep.astype(jnp.bfloat16), "depth", split_axis=1, concat_axis=2, tiled=True
    ).astype(blurred_deep.dtype)
    correction = covered[:, None, :, None] * (views.astype(jnp.float32) / blurred - 1.0)
    correction_deep = lax.all_to_all(
        correction.astype(jnp.bfloat16), "depth", split_axis=2, concat_axis=1, tiled=True
    ).astype(correction.dtype)
    backward_deep = convolve(correction_deep, flipped_z, 1)
    backward = lax.all_to_all(
        backward_deep.astype(jnp.bfloat16), "depth", split_axis=1, concat_axis=2, tiled=True
    ).astype(backward_deep.dtype)
    backward = convolve(backward, flipped_y, 3)
    widened_back = extended(backward.astype(jnp.bfloat16), (("tile", 2),), margin).astype(
        backward.dtype
    )
    summed = jnp.sum(strip_pass(widened_back, flipped_x, strip_rows, 2), axis=0)
    return estimate * (1.0 + summed / jnp.maximum(coverage, 1.0)[None, :, None])


def solution(mesh):
    in_specs = (P("depth", "tile", None), P(None, "depth", "tile", None), P(), P(), P(), P())
    out_specs = P("depth", "tile", None)
    return jax.shard_map(shards, mesh=mesh, in_specs=in_specs, out_specs=out_specs, check_vma=False)
```

profile of v0, /device:TPU:1, one launch (start us, length us, event | category | flops | bytes accessed | tf_op | source)
XLA Modules:
  0.0 211.2 jit_solution(2465363015208391881)
XLA Ops:
  0.0 1.0 convert_element_type.97
  1.0 4.5 %collective-permute-start = (bf16[2,15,1024]{2,1,0:T(8,128)(2,1)S(1)}, bf16[2,15,1024]{2,1,0:T(8,128)(2,1)S(1)}, u32[]{:S(2)}, u32[]{:S(2)}) collective-permute-start(bf16[2,15,1024]{2,1,0:T(8,128)(2,1)S(1)} %get-tuple-element.131), channel_id=1, source_target_pairs={{0,4},{4,8},{8,12},{12,16},{16,20},{20,24},{24,28},{1,5},{5,9},{9,... | collective-permute-start | bytes 184328 | tf_op jit(solution)/shard_map/ppermute | solution.py:14
  5.5 1.9 collective-permute-start.1
  7.4 1.0 convert_bitcast_fusion.4
  8.4 0.8 reduce_sum.45
  9.2 0.8 broadcast_divide_fusion.2
  10.0 0.5 slice_reduce_fusion.76
  10.5 0.4 slice_reduce_fusion.71
  10.8 0.8 reduce_sum.46
  11.7 0.8 broadcast_divide_fusion.1
  12.4 0.5 slice_reduce_fusion.75
  12.9 0.4 slice_reduce_fusion.72
  13.3 0.0 collective-permute-done
  13.3 0.0 collective-permute-done.1
  13.3 0.1 maximum_convert_fusion.1
  13.4 0.6 slice_bitcast_fusion.30
  14.0 0.4 slice_bitcast_fusion.29
  14.4 5.2 %multiply_add_fusion = f32[8,2,32,1024]{3,2,1,0:T(8,128)S(1)} fusion(f32[2,32,1024]{2,1,0:T(8,128)S(1)} %get-tuple-element.101, f32[2,32,1024]{2,1,0:T(8,128)S(1)} %get-tuple-element.102, f32[8]{0:T(128)S(1)} %get-tuple-element.68, f32[2,32,1024]{2,1,0:T(8,128)S(1)} %get-tuple-element.103, f32[8]{0:T(128)S(1)} %get-tuple-element.69, ...), kind=kLoop, calls=%fused_computation.342 | loop fusion | flops 31981568 | bytes 10224608 | tf_op jit(solution)/shard_map/add | solution.py:48
  19.6 17.1 %fusion.54 = bf16[8,2,32,1024]{3,2,1,0:T(8,128)(2,1)S(1)} fusion(f32[8,2,32,1024]{3,2,1,0:T(8,128)S(1)} %multiply_add_fusion, f32[8]{0:T(128)S(1)} %get-tuple-element.37, f32[8]{0:T(128)S(1)} %get-tuple-element.38, f32[8]{0:T(128)S(1)} %get-tuple-element.39, f32[8]{0:T(128)S(1)} %get-tuple-element.40, f32[8]{0:T(128)S(1)} %get-tuple-element.41, ...), kind=kLoop, calls=%fused_computation.142 | loop fusion | flops 32505856 | bytes 3146720 | tf_op jit(solution)/shard_map/convert_element_type | solution.py:76
  36.7 0.0 copy-start.2
  36.7 2.1 copy.11
  38.8 4.6 %all-to-all-start = ((bf16[8,2,32,1024]{3,1,0,2:T(2,128)(2,1)}), bf16[8,2,32,1024]{3,1,0,2:T(2,128)(2,1)S(1)}, u32[]{:S(2)}, u32[]{:S(2)}) async-start(bf16[8,2,32,1024]{3,1,0,2:T(2,128)(2,1)} %copy.11), calls=%async_computation | async-start | bytes 2097152 | tf_op jit(solution)/shard_map/all_to_all | solution.py:75
  43.4 0.0 copy-done.2
  43.4 0.1 reduce_sum.47
  43.5 0.1 broadcast_divide_fusion
  43.5 0.4 multiply_reduce_fusion.6
  43.9 0.5 slice_reduce_fusion.74
  44.4 23.7 %all-to-all-done = bf16[8,2,32,1024]{3,1,0,2:T(2,128)(2,1)S(1)} async-done(((bf16[8,2,32,1024]{3,1,0,2:T(2,128)(2,1)}), bf16[8,2,32,1024]{3,1,0,2:T(2,128)(2,1)S(1)}, u32[]{:S(2)}, u32[]{:S(2)}) %all-to-all-start) | async-done | bytes 1048608 | tf_op jit(solution)/shard_map/all_to_all | solution.py:75
  68.2 0.6 convert_bitcast_fusion.3
  68.8 0.1 copy.13
  69.0 2.9 %add_convert_fusion.1 = bf16[8,8,8,1024]{3,2,1,0:T(8,128)(2,1)S(1)} fusion(f32[8,8,8,1024]{3,2,1,0:T(8,128)S(1)} %bitcast.99, f32[8]{0:T(128)S(1)} %get-tuple-element.35, f32[8]{0:T(128)S(1)} %get-tuple-element.34, f32[8]{0:T(128)S(1)} %get-tuple-element.33, f32[8]{0:T(128)S(1)} %get-tuple-element.32, f32[8]{0:T(128)S(1)} %get-tuple-element.31, ...), kind=kLoop, calls=%fused_computation.341 | loop fusion | flops 20447232 | bytes 3146496 | tf_op jit(solution)/shard_map/convert_element_type | solution.py:80
  71.9 0.0 copy-start.3
  71.9 1.1 copy.14
  73.0 0.0 copy-start.1
  73.0 3.6 %all-to-all-start.1 = ((bf16[8,8,8,1024]{3,2,0,1:T(8,128)(2,1)}), bf16[8,8,8,1024]{3,2,0,1:T(8,128)(2,1)S(1)}, u32[]{:S(2)}, u32[]{:S(2)}) async-start(bf16[8,8,8,1024]{3,2,0,1:T(8,128)(2,1)} %copy.14), calls=%async_computation.1 | async-start | bytes 2097152 | tf_op jit(solution)/shard_map/all_to_all | solution.py:79
  76.6 0.0 copy-done.3
  76.7 0.1 and_convert_fusion
  76.7 26.0 %all-to-all-done.1 = bf16[8,8,8,1024]{3,2,0,1:T(8,128)(2,1)S(1)} async-done(((bf16[8,8,8,1024]{3,2,0,1:T(8,128)(2,1)}), bf16[8,8,8,1024]{3,2,0,1:T(8,128)(2,1)S(1)}, u32[]{:S(2)}, u32[]{:S(2)}) %all-to-all-start.1) | async-done | bytes 1048608 | tf_op jit(solution)/shard_map/all_to_all | solution.py:79
  102.7 0.1 copy.15
  102.8 0.0 copy-done.1
  102.8 0.6 fusion.213
  103.4 2.1 copy.17
  105.5 3.5 %all-to-all-start.2 = ((bf16[8,2,32,1024]{3,1,0,2:T(2,128)(2,1)}), bf16[8,2,32,1024]{3,1,0,2:T(2,128)(2,1)S(1)}, u32[]{:S(2)}, u32[]{:S(2)}) async-start(bf16[8,2,32,1024]{3,1,0,2:T(2,128)(2,1)} %copy.17), calls=%async_computation.2 | async-start | bytes 2097152 | tf_op jit(solution)/shard_map/all_to_all | solution.py:83
  109.1 25.3 %all-to-all-done.2 = bf16[8,2,32,1024]{3,1,0,2:T(2,128)(2,1)S(1)} async-done(((bf16[8,2,32,1024]{3,1,0,2:T(2,128)(2,1)}), bf16[8,2,32,1024]{3,1,0,2:T(2,128)(2,1)S(1)}, u32[]{:S(2)}, u32[]{:S(2)}) %all-to-all-start.2) | async-done | bytes 1048608 | tf_op jit(solution)/shard_map/all_to_all | solution.py:83
  134.3 0.6 convert_bitcast_fusion.1
  134.9 0.1 copy.19
  135.1 2.9 %add_convert_fusion = bf16[8,8,8,1024]{3,2,1,0:T(8,128)(2,1)S(1)} fusion(f32[8,8,8,1024]{3,2,1,0:T(8,128)S(1)} %bitcast.98, f32[8]{0:T(128)S(1)} %get-tuple-element.27, f32[8]{0:T(128)S(1)} %get-tuple-element.24, f32[8]{0:T(128)S(1)} %get-tuple-element.26, f32[8]{0:T(128)S(1)} %get-tuple-element.25, f32[8]{0:T(128)S(1)} %get-tuple-element.23, ...), kind=kLoop, calls=%fused_computation.340 | loop fusion | flops 20447232 | bytes 3146496 | tf_op jit(solution)/shard_map/convert_element_type | solution.py:88
  138.0 0.1 copy.20
  138.1 27.2 %all_to_all.16 = bf16[8,8,8,1024]{3,2,0,1:T(8,128)(2,1)S(1)} all-to-all(bf16[8,8,8,1024]{3,2,0,1:T(8,128)(2,1)S(1)} %copy.20), channel_id=1, replica_groups=mesh['tile'=8,'depth'=4] {'depth'}, dimensions={1} | all-to-all | bytes 2097152 | tf_op jit(solution)/shard_map/all_to_all | solution.py:87
  165.3 0.1 copy.21
  165.4 0.2 copy_bitcast_fusion
  165.6 16.9 %fusion.115 = bf16[8,2,32,1024]{3,2,1,0:T(8,128)(2,1)S(1)} fusion(f32[8,2,32,1024]{3,2,1,0:T(8,128)S(1)} %copy_bitcast_fusion, f32[8]{0:T(128)S(1)} %get-tuple-element.37, f32[8]{0:T(128)S(1)} %get-tuple-element.38, f32[8]{0:T(128)S(1)} %get-tuple-element.39, f32[8]{0:T(128)S(1)} %get-tuple-element.40, f32[8]{0:T(128)S(1)} %get-tuple-element.41, ...), kind=kLoop, calls=%fused_computation.203 | loop fusion | flops 32505856 | bytes 3146720 | tf_op jit(solution)/shard_map/convert_element_type | solution.py:91
  182.6 0.2 fusion.215
  182.8 4.3 %collective-permute-start.2 = (bf16[8,2,15,1024]{3,2,1,0:T(8,128)(2,1)S(1)}, bf16[8,2,15,1024]{3,2,1,0:T(8,128)(2,1)S(1)}, u32[]{:S(2)}, u32[]{:S(2)}) collective-permute-start(bf16[8,2,15,1024]{3,2,1,0:T(8,128)(2,1)S(1)} %get-tuple-element.98), channel_id=1, source_target_pairs={{0,4},{4,8},{8,12},{12,16},{16,20},{20,24},{24,28},{1,5},{5,9},{9,... | collective-permute-start | bytes 1474568 | tf_op jit(solution)/shard_map/ppermute | solution.py:14
  187.1 1.9 collective-permute-start.3
  189.0 0.1 fusion.214
  189.1 4.1 %collective-permute-done.2 = bf16[8,2,15,1024]{3,2,1,0:T(8,128)(2,1)S(1)} collective-permute-done((bf16[8,2,15,1024]{3,2,1,0:T(8,128)(2,1)S(1)}, bf16[8,2,15,1024]{3,2,1,0:T(8,128)(2,1)S(1)}, u32[]{:S(2)}, u32[]{:S(2)}) %collective-permute-start.2) | collective-permute-done | bytes 491552 | tf_op jit(solution)/shard_map/ppermute | solution.py:14
  193.2 7.3 %collective-permute-done.3 = bf16[8,2,15,1024]{3,2,1,0:T(8,128)(2,1)S(1)} collective-permute-done((bf16[8,2,15,1024]{3,2,1,0:T(8,128)(2,1)S(1)}, bf16[8,2,15,1024]{3,2,1,0:T(8,128)(2,1)S(1)}, u32[]{:S(2)}, u32[]{:S(2)}) %collective-permute-start.3) | collective-permute-done | bytes 491552 | tf_op jit(solution)/shard_map/ppermute | solution.py:15
  200.4 0.7 maximum_convert_fusion
  201.1 0.0 copy-start
  201.1 9.2 %fusion.181 = f32[2,32,1024]{2,1,0:T(8,128)S(1)} fusion(f32[8,2,62,1024]{3,2,1,0:T(8,128)S(1)} %maximum_convert_fusion, f32[8]{0:T(128)S(1)} %get-tuple-element.68, f32[8]{0:T(128)S(1)} %get-tuple-element.69, f32[8]{0:T(128)S(1)} %get-tuple-element.70, f32[8]{0:T(128)S(1)} %get-tuple-element.71, f32[8]{0:T(128)S(1)} %get-tuple-element.72, ...), kind=kLoop, calls=%fused_computation.270 | loop fusion | flops 32440320 | bytes 65274848 | tf_op jit(solution)/shard_map/reduce_sum | solution.py:94
  210.4 0.0 copy-done
  210.4 0.8 add_multiply_fusion
  (6 shorter events, 0.1 us)
Async XLA Ops:
  1.0 12.3 %collective-permute-start = (bf16[2,15,1024]{2,1,0:T(8,128)(2,1)S(1)}, bf16[2,15,1024]{2,1,0:T(8,128)(2,1)S(1)}, u32[]{:S(2)}, u32[]{:S(2)}) collective-permute-start(bf16[2,15,1024]{2,1,0:T(8,128)(2,1)S(1)} %get-tuple-element.131), channel_id=1, source_target_pairs={{0,4},{4,8},{8,12},{12,16},{16,20},{20,24},{24,28},{1,5},{5,9},{9,... | collective-permute-start | bytes 184328 | tf_op jit(solution)/shard_map/ppermute | solution.py:14
  5.5 7.8 %collective-permute-start.1 = (bf16[2,15,1024]{2,1,0:T(8,128)(2,1)S(1)}, bf16[2,15,1024]{2,1,0:T(8,128)(2,1)S(1)}, u32[]{:S(2)}, u32[]{:S(2)}) collective-permute-start(bf16[2,15,1024]{2,1,0:T(8,128)(2,1)S(1)} %get-tuple-element.132), channel_id=1, source_target_pairs={{4,0},{8,4},{12,8},{16,12},{20,16},{24,20},{28,24},{5,1},{9,5},{13... | collective-permute-start | bytes 184328 | tf_op jit(solution)/shard_map/ppermute | solution.py:15
  36.7 6.7 %copy-start.2 = (f32[8,31]{1,0:T(8,128)S(1)}, f32[8,31]{1,0:T(8,128)}, u32[]{:S(2)}) copy-start(f32[8,31]{1,0:T(8,128)} %param.10) | copy-start | bytes 2980
  38.8 29.4 %all-to-all-start = ((bf16[8,2,32,1024]{3,1,0,2:T(2,128)(2,1)}), bf16[8,2,32,1024]{3,1,0,2:T(2,128)(2,1)S(1)}, u32[]{:S(2)}, u32[]{:S(2)}) async-start(bf16[8,2,32,1024]{3,1,0,2:T(2,128)(2,1)} %copy.11), calls=%async_computation | async-start | bytes 2097152 | tf_op jit(solution)/shard_map/all_to_all | solution.py:75
  71.9 4.8 %copy-start.3 = (s32[8]{0:T(128)S(1)}, s32[8]{0:T(128)}, u32[]{:S(2)}) copy-start(s32[8]{0:T(128)} %param.11) | copy-start | bytes 100
  73.0 29.9 %copy-start.1 = (bf16[8,2,32,1024]{3,2,1,0:T(8,128)(2,1)S(1)}, bf16[8,2,32,1024]{3,2,1,0:T(8,128)(2,1)}, u32[]{:S(2)}) copy-start(bf16[8,2,32,1024]{3,2,1,0:T(8,128)(2,1)} %param.7) | copy-start | bytes 3145732
  73.0 29.8 %all-to-all-start.1 = ((bf16[8,8,8,1024]{3,2,0,1:T(8,128)(2,1)}), bf16[8,8,8,1024]{3,2,0,1:T(8,128)(2,1)S(1)}, u32[]{:S(2)}, u32[]{:S(2)}) async-start(bf16[8,8,8,1024]{3,2,0,1:T(8,128)(2,1)} %copy.14), calls=%async_computation.1 | async-start | bytes 2097152 | tf_op jit(solution)/shard_map/all_to_all | solution.py:79
  105.5 28.8 %all-to-all-start.2 = ((bf16[8,2,32,1024]{3,1,0,2:T(2,128)(2,1)}), bf16[8,2,32,1024]{3,1,0,2:T(2,128)(2,1)S(1)}, u32[]{:S(2)}, u32[]{:S(2)}) async-start(bf16[8,2,32,1024]{3,1,0,2:T(2,128)(2,1)} %copy.17), calls=%async_computation.2 | async-start | bytes 2097152 | tf_op jit(solution)/shard_map/all_to_all | solution.py:83
  182.8 10.4 %collective-permute-start.2 = (bf16[8,2,15,1024]{3,2,1,0:T(8,128)(2,1)S(1)}, bf16[8,2,15,1024]{3,2,1,0:T(8,128)(2,1)S(1)}, u32[]{:S(2)}, u32[]{:S(2)}) collective-permute-start(bf16[8,2,15,1024]{3,2,1,0:T(8,128)(2,1)S(1)} %get-tuple-element.98), channel_id=1, source_target_pairs={{0,4},{4,8},{8,12},{12,16},{16,20},{20,24},{24,28},{1,5},{5,9},{9,... | collective-permute-start | bytes 1474568 | tf_op jit(solution)/shard_map/ppermute | solution.py:14
  187.1 13.4 %collective-permute-start.3 = (bf16[8,2,15,1024]{3,2,1,0:T(8,128)(2,1)S(1)}, bf16[8,2,15,1024]{3,2,1,0:T(8,128)(2,1)S(1)}, u32[]{:S(2)}, u32[]{:S(2)}) collective-permute-start(bf16[8,2,15,1024]{3,2,1,0:T(8,128)(2,1)S(1)} %get-tuple-element.99), channel_id=1, source_target_pairs={{4,0},{8,4},{12,8},{16,12},{20,16},{24,20},{28,24},{5,1},{9,5},{13... | collective-permute-start | bytes 1474568 | tf_op jit(solution)/shard_map/ppermute | solution.py:15
  201.1 9.2 %copy-start = (f32[2,32,1024]{2,1,0:T(8,128)S(1)}, f32[2,32,1024]{2,1,0:T(8,128)}, u32[]{:S(2)}) copy-start(f32[2,32,1024]{2,1,0:T(8,128)} %param.6) | copy-start | bytes 786436
where the time goes:
time: 212 us; the launch traced here: 211 us
  waiting for transfers between devices  86.3 us (41%)
  other arithmetic  64.2 us (30%)
  blocking collectives  27.2 us (13%)
  starting transfers between devices  24.4 us (12%)
  local copies, waits for them, and re-layouts  8.7 us (4%)
    all_to_all x1, blocking collectives, shards(): lax.all_to_all(backward_deep.astype(jnp.bfloat16), 'depth', split_axis=1,...  27.2 us
    all_to_all x1, waiting for transfers between devices, shards(): lax.all_to_all(blurred_deep.astype(jnp.bfloat16), 'depth', split_axis=1,...  26 us
    all_to_all x1, waiting for transfers between devices, shards(): lax.all_to_all(correction.astype(jnp.bfloat16), 'depth', split_axis=2, co...  25.3 us
    all_to_all x1, waiting for transfers between devices, shards(): lax.all_to_all(partial_blur.astype(jnp.bfloat16), 'depth', split_axis=2,...  23.7 us
    convert_element_type x1, other arithmetic, shards(): partial_blur.astype(jnp.bfloat16)  17.1 us
    convert_element_type x1, other arithmetic, shards(): backward.astype(jnp.bfloat16)  16.9 us
    reduce_sum x1, other arithmetic, shards(): summed = jnp.sum(strip_pass(widened_back, flipped_x, strip_rows, 2), axis=0)  9.22 us
    ppermute x2, starting transfers between devices, extended(): before = lax.ppermute(last, axis, up)  8.82 us
  transfers between devices with their start and end apart: 7, of which 5 were waited for; matrix products, arithmetic and copies ran while one was open for 3% of the time, Pallas kernels for 0%

commit v1 on v0

v1 whole, which is shorter than its diff:
```python
import functools
import jax
import jax.numpy as jnp
from jax import lax
from jax.experimental import pallas as pl
from jax.experimental.pallas import tpu as pltpu
from jax.sharding import PartitionSpec as P

F32, BF16 = jnp.float32, jnp.bfloat16
HALO = 16
LANES = 128
WIDE = 256
VMEM_LIMIT = 40 * 1024 * 1024


def normalized(ref):
    return ref[...] / jnp.sum(ref[...], axis=1, keepdims=True)


def select_taps(index, kernel):
    total = jnp.zeros((kernel.shape[0],) + index.shape[1:], F32)
    for tap in range(kernel.shape[1]):
        total = total + jnp.where(index == tap, kernel[:, tap : tap + 1], 0.0)
    return total


def slanted(row, rows):
    spread = jnp.broadcast_to(row, (rows, row.shape[1]))
    return pltpu.roll(spread, 0, 1, stride=1, stride_axis=0)


def matrices_kernel(planes, strip, depth_ref, kx_ref, ky_ref, kz_ref, w_ref, wt_ref, tf_ref, tb_ref):
    views, taps = kx_ref.shape
    margin = taps // 2
    extent = strip + 2 * HALO
    depth = w_ref.shape[1] // (planes * extent)
    kx, ky, kz = normalized(kx_ref), normalized(ky_ref), normalized(kz_ref)
    lane = lax.broadcasted_iota(jnp.int32, (1, LANES), 1)
    x_row = select_taps(lane % extent - (HALO - margin), kx)
    near = jnp.where(lane < LANES // 2, lane, lane - LANES)
    forward_row = select_taps(margin - near, ky)
    backward_row = select_taps(margin + near, ky)
    column = lax.broadcasted_iota(jnp.int32, (1, w_ref.shape[1]), 1) // extent
    device = depth_ref[0]
    source = device + column // planes
    source = jnp.where(source >= depth, source - depth, source)
    plane = source * planes + column % planes
    z_rows = [select_taps(plane - (device * planes + own) + margin, kz) for own in range(planes)]
    for view in range(views):
        x_block = slanted(x_row[view : view + 1], strip)
        x_block = jnp.concatenate([x_block] * (w_ref.shape[1] // LANES), axis=1)
        for own in range(planes):
            first = (view * planes + own) * strip
            block = x_block * z_rows[own][view : view + 1]
            w_ref[first : first + strip, :] = block.astype(BF16)
    wt_ref[...] = w_ref[...].astype(F32).T.astype(BF16)
    i = lax.broadcasted_iota(jnp.int32, (LANES, LANES), 0)
    j = lax.broadcasted_iota(jnp.int32, (LANES, LANES), 1)
    zeros = jnp.zeros((LANES, LANES), BF16)
    for view in range(views):
        for row, out in ((forward_row, tf_ref), (backward_row, tb_ref)):
            circle = slanted(row[view : view + 1], LANES)
            middle = jnp.where(jnp.abs(j - i) < LANES // 2, circle, 0.0).astype(BF16)
            earlier = jnp.where(i - j > LANES // 2, circle, 0.0).astype(BF16)
            later = jnp.where(j - i > LANES // 2, circle, 0.0).astype(BF16)
            grid = ((earlier, zeros), (middle, earlier), (later, middle), (zeros, later))
            for a, blocks in enumerate(grid):
                for b, block in enumerate(blocks):
                    out[view, a * LANES : (a + 1) * LANES, b * LANES : (b + 1) * LANES] = block


def write_coded(out_ref, where, values):
    pick = values.shape[-1] // 2 - LANES
    base = values[..., pick : pick + LANES].astype(BF16)
    wide = base.astype(F32)
    for first in range(0, values.shape[-1], LANES):
        part = values[..., first : first + LANES]
        part = base if first == pick else (part - wide).astype(BF16)
        out_ref[where + (slice(first, first + LANES),)] = part


def decoded(values, first):
    pick = values.shape[-1] // 2 - LANES
    base = values[..., pick : pick + LANES].astype(F32)
    if first == pick:
        return base
    return base + values[..., first : first + LANES].astype(F32)


def main_kernel(planes, strip, view_rows, place_ref, offsets_ref, *refs):
    (all_ref, before_ref, after_ref, views_ref, w_ref, wt_ref, tf_ref, tb_ref,
     core_ref, top_ref, bottom_ref, ext_ref, pad_ref, back_ref, deep_ref) = refs
    views = offsets_ref.shape[0]
    extent = strip + 2 * HALO
    columns = all_ref.shape[-1]
    group = planes * strip
    for p in range(all_ref.shape[0]):
        first = p * extent
        ext_ref[first : first + HALO, :] = before_ref[p]
        ext_ref[first + HALO : first + HALO + strip, :] = all_ref[p]
        ext_ref[first + HALO + strip : first + extent, :] = after_ref[p]
    for pad in (pad_ref, back_ref):
        pad[:, :LANES] = jnp.zeros((pad.shape[0], LANES), BF16)
        pad[:, LANES + columns :] = jnp.zeros((pad.shape[0], LANES), BF16)
    for first in range(0, columns, WIDE):
        block = jnp.dot(w_ref[...], ext_ref[:, first : first + WIDE], preferred_element_type=F32)
        pad_ref[:, LANES + first : LANES + first + WIDE] = block.astype(BF16)
    row = place_ref[0] + lax.broadcasted_iota(jnp.int32, (group, WIDE), 0) % strip
    starts = range(0, columns, WIDE)

    def windows(pad, rows):
        return jnp.concatenate([pad[rows, first : first + WIDE + 2 * LANES] for first in starts], axis=0)

    for view in range(views):
        rows = slice(view * group, (view + 1) * group)
        low = offsets_ref[view]
        inside = (row >= low) & (row < low + view_rows)
        blurred = jnp.dot(windows(pad_ref, rows), tf_ref[view], preferred_element_type=F32)
        for n, first in enumerate(starts):
            part = blurred[n * group : (n + 1) * group]
            seen = views_ref[rows, first : first + WIDE].astype(F32)
            correction = jnp.where(inside, seen / part - 1.0, 0.0)
            back_ref[rows, LANES + first : LANES + first + WIDE] = correction.astype(BF16)
        backward = jnp.dot(windows(back_ref, rows), tb_ref[view], preferred_element_type=F32)
        for n, first in enumerate(starts):
            deep_ref[rows, first : first + WIDE] = backward[n * group : (n + 1) * group].astype(BF16)
    for p in range(core_ref.shape[0]):
        part = jnp.dot(wt_ref[p * extent : (p + 1) * extent], deep_ref[...], preferred_element_type=F32)
        core_ref[p] = part[HALO : HALO + strip]
        write_coded(top_ref, (p, slice(None)), part[:HALO])
        write_coded(bottom_ref, (p, slice(None)), part[HALO + strip :])


def join_kernel(planes, core_ref, above_ref, below_ref, own_ref, *sends):
    strip = core_ref.shape[1]
    columns = core_ref.shape[2]
    for p in range(core_ref.shape[0]):
        above, below = above_ref[p], below_ref[p]
        parts = []
        for first in range(0, columns, LANES):
            lanes = slice(first, first + LANES)
            tail = core_ref[p, strip - HALO :, lanes] + decoded(below, first)
            head = core_ref[p, :HALO, lanes] + decoded(above, first)
            inner = [core_ref[p, HALO : strip - HALO, lanes]] if strip > 2 * HALO else []
            parts.append(jnp.concatenate([head, *inner, tail], axis=0))
        whole = jnp.concatenate(parts, axis=1)
        if p < planes:
            own_ref[p] = whole
        else:
            write_coded(sends[p // planes - 1], (p % planes, slice(None)), whole)


def update_kernel(view_rows, place_ref, offsets_ref, estimate_ref, own_ref, *refs):
    received, out_ref = refs[:-1], refs[-1]
    planes, strip, columns = estimate_ref.shape
    row = place_ref[0] + lax.broadcasted_iota(jnp.int32, (strip, LANES), 0)
    coverage = jnp.zeros((strip, LANES), F32)
    for view in range(offsets_ref.shape[0]):
        low = offsets_ref[view]
        coverage = coverage + jnp.where((row >= low) & (row < low + view_rows), 1.0, 0.0)
    scale = 1.0 / jnp.maximum(coverage, 1.0)
    for p in range(planes):
        for first in range(0, columns, LANES):
            lanes = slice(first, first + LANES)
            summed = own_ref[p, :, lanes]
            for ref in received:
                summed = summed + decoded(ref[p], first)
            out_ref[p, :, lanes] = estimate_ref[p, :, lanes] * (1.0 + summed * scale)


def call(body, outs, scalars, arrays, scratch=(), flops=0, moved=0):
    return pl.pallas_call(
        body,
        out_shape=outs,
        in_specs=[pl.BlockSpec(memory_space=pltpu.SMEM)] * scalars
        + [pl.BlockSpec(memory_space=pltpu.VMEM)] * arrays,
        out_specs=jax.tree.map(lambda _: pl.BlockSpec(memory_space=pltpu.VMEM), outs),
        scratch_shapes=list(scratch),
        compiler_params=pltpu.CompilerParams(vmem_limit_bytes=VMEM_LIMIT),
        cost_estimate=pl.CostEstimate(flops=flops, bytes_accessed=moved, transcendentals=0),
    )


def shards(estimate, views, kernel_x, kernel_y, kernel_z, offsets):
    shape = jax.ShapeDtypeStruct
    depth, tiles = lax.axis_size("depth"), lax.axis_size("tile")
    planes, strip, columns = estimate.shape
    count = views.shape[0]
    extent = strip + 2 * HALO
    rows = count * planes * strip
    deep = depth * planes
    inner = deep * extent
    view_rows = 5 * strip * tiles // 8
    place = (lax.axis_index("tile") * strip).astype(jnp.int32).reshape(1)
    device = lax.axis_index("depth").astype(jnp.int32).reshape(1)

    def turned(array, shift):
        return lax.ppermute(array, "depth", [(i, (i - shift) % depth) for i in range(depth)])

    up = [(i, i + 1) for i in range(tiles - 1)]
    down = [(j, i) for i, j in up]

    own = estimate.astype(BF16)
    chunks = [own] + [turned(own, shift) for shift in range(1, depth)]
    w, wt, tf, tb = call(
        functools.partial(matrices_kernel, planes, strip),
        (shape((rows, inner), BF16), shape((inner, rows), BF16))
        + (shape((count, WIDE + 2 * LANES, WIDE), BF16),) * 2,
        1, 3, flops=10**8, moved=5 * 2**20,
    )(device, kernel_x, kernel_y, kernel_z)
    gathered = jnp.concatenate(chunks, axis=0)
    before = lax.ppermute(gathered[:, strip - HALO :], "tile", up)
    after = lax.ppermute(gathered[:, :HALO], "tile", down)
    halo = shape((deep, HALO, columns), BF16)
    core, top, bottom = call(
        functools.partial(main_kernel, planes, strip, view_rows),
        (shape((deep, strip, columns), F32), halo, halo),
        2, 8,
        scratch=(
            pltpu.VMEM((inner, columns), BF16),
            pltpu.VMEM((rows, columns + 2 * LANES), BF16),
            pltpu.VMEM((rows, columns + 2 * LANES), BF16),
            pltpu.VMEM((rows, columns), BF16),
        ),
        flops=2 * 10**9, moved=10 * 2**20,
    )(place, offsets, gathered, before, after, views.reshape(rows, columns), w, wt, tf, tb)
    below = lax.ppermute(top, "tile", down)
    above = lax.ppermute(bottom, "tile", up)
    block = (planes, strip, columns)
    own_sum, *sends = call(
        functools.partial(join_kernel, planes),
        (shape(block, F32),) + (shape(block, BF16),) * (depth - 1),
        0, 3, flops=10**6, moved=3 * 2**20,
    )(core, above, below)
    received = [turned(send, depth - 1 - n) for n, send in enumerate(sends)]
    return call(
        functools.partial(update_kernel, view_rows),
        shape(block, F32),
        2, 2 + len(received), flops=10**6, moved=2**20,
    )(place, offsets, estimate, own_sum, *received)


def solution(mesh):
    in_specs = (P("depth", "tile", None), P(None, "depth", "tile", None), P(), P(), P(), P())
    out_specs = P("depth", "tile", None)
    return jax.shard_map(shards, mesh=mesh, in_specs=in_specs, out_specs=out_specs, check_vma=False)
```

time: 212 us -> 56.8 us (0.27)
  the two profiles are of different devices: /device:TPU:1 before, /device:TPU:11 now
where the time goes in v1:
time: 56.8 us; the launch traced here: 56.6 us
  waiting for transfers between devices  29.5 us (52%)
  starting transfers between devices  19.3 us (34%)
  Pallas kernels  6.52 us (11%)
  other arithmetic  1.12 us (2%)
    ppermute x6, waiting for transfers between devices, turned(): lax.ppermute(array, 'depth', [(i, (i - shift) % depth) for i in range(dep...  20.6 us
    ppermute x6, starting transfers between devices, turned(): lax.ppermute(array, 'depth', [(i, (i - shift) % depth) for i in range(dep...  5.65 us
    ppermute x1, starting transfers between devices, shards(): above = lax.ppermute(bottom, 'tile', up)  5.29 us
    ppermute x1, starting transfers between devices, shards(): before = lax.ppermute(gathered[:, strip - HALO:], 'tile', up)  4.06 us
    pallas_call x1, Pallas kernels, shards(): call(functools.partial(main_kernel, planes, strip, view_rows), (shape((de...  3.9 us
    ppermute x1, waiting for transfers between devices, shards(): below = lax.ppermute(top, 'tile', down)  3.42 us
    ppermute x1, waiting for transfers between devices, shards(): above = lax.ppermute(bottom, 'tile', up)  3.24 us
    ppermute x1, starting transfers between devices, shards(): after = lax.ppermute(gathered[:, :HALO], 'tile', down)  2.4 us
  transfers between devices with their start and end apart: 10, of which 10 were waited for; matrix products, arithmetic and copies ran while one was open for 0% of the time, Pallas kernels for 2%

profile of v1, /device:TPU:11, one launch (start us, length us, event | category | flops | bytes accessed | tf_op | source)
XLA Modules:
  0.0 56.6 jit_solution(16684445469088373898)
XLA Ops:
  0.0 0.0 copy-start.5
  0.0 0.0 copy-start.4
  0.0 0.0 copy-start.3
  0.0 0.0 copy-start.1
  0.0 0.0 copy-start.2
  0.0 1.1 %convert_element_type.3 = bf16[2,32,1024]{2,1,0:T(8,128)(2,1)S(1)} convert(f32[2,32,1024]{2,1,0:T(8,128)} %estimate_ref.1) | non-fusion elementwise | flops 65536 | bytes 393216 | tf_op jit(solution)/shard_map/convert_element_type | solution.py:203
  1.1 1.3 %collective-permute-start.2 = (bf16[2,32,1024]{2,1,0:T(8,128)(2,1)S(1)}, bf16[2,32,1024]{2,1,0:T(8,128)(2,1)S(1)}, u32[]{:S(2)}, u32[]{:S(2)}) collective-permute-start(bf16[2,32,1024]{2,1,0:T(8,128)(2,1)S(1)} %convert_element_type.3), channel_id=1, source_target_pairs={{0,1},{1,2},{2,3},{3,0},{4,5},{5,6},{6,7},{7,4},{8,9},{9,10},{10,1... | collective-permute-start | bytes 393224 | tf_op jit(solution)/shard_map/ppermute | solution.py:198
  2.4 1.1 %collective-permute-start.1 = (bf16[2,32,1024]{2,1,0:T(8,128)(2,1)S(1)}, bf16[2,32,1024]{2,1,0:T(8,128)(2,1)S(1)}, u32[]{:S(2)}, u32[]{:S(2)}) collective-permute-start(bf16[2,32,1024]{2,1,0:T(8,128)(2,1)S(1)} %convert_element_type.3), channel_id=1, source_target_pairs={{0,2},{1,3},{2,0},{3,1},{4,6},{5,7},{6,4},{7,5},{8,10},{9,11},{10,... | collective-permute-start | bytes 393224 | tf_op jit(solution)/shard_map/ppermute | solution.py:198
  3.5 1.4 %collective-permute-start = (bf16[2,32,1024]{2,1,0:T(8,128)(2,1)S(1)}, bf16[2,32,1024]{2,1,0:T(8,128)(2,1)S(1)}, u32[]{:S(2)}, u32[]{:S(2)}) collective-permute-start(bf16[2,32,1024]{2,1,0:T(8,128)(2,1)S(1)} %convert_element_type.3), channel_id=1, source_target_pairs={{0,3},{1,0},{2,1},{3,2},{4,7},{5,4},{6,5},{7,6},{8,11},{9,8},{10,9... | collective-permute-start | bytes 393224 | tf_op jit(solution)/shard_map/ppermute | solution.py:198
  4.9 0.6 %collective-permute-done.2 = bf16[2,32,1024]{2,1,0:T(8,128)(2,1)S(1)} collective-permute-done((bf16[2,32,1024]{2,1,0:T(8,128)(2,1)S(1)}, bf16[2,32,1024]{2,1,0:T(8,128)(2,1)S(1)}, u32[]{:S(2)}, u32[]{:S(2)}) %collective-permute-start.2) | collective-permute-done | bytes 131104 | tf_op jit(solution)/shard_map/ppermute | solution.py:198
  5.5 7.5 %collective-permute-done.1 = bf16[2,32,1024]{2,1,0:T(8,128)(2,1)S(1)} collective-permute-done((bf16[2,32,1024]{2,1,0:T(8,128)(2,1)S(1)}, bf16[2,32,1024]{2,1,0:T(8,128)(2,1)S(1)}, u32[]{:S(2)}, u32[]{:S(2)}) %collective-permute-start.1) | collective-permute-done | bytes 131104 | tf_op jit(solution)/shard_map/ppermute | solution.py:198
  13.0 2.8 %collective-permute-done = bf16[2,32,1024]{2,1,0:T(8,128)(2,1)S(1)} collective-permute-done((bf16[2,32,1024]{2,1,0:T(8,128)(2,1)S(1)}, bf16[2,32,1024]{2,1,0:T(8,128)(2,1)S(1)}, u32[]{:S(2)}, u32[]{:S(2)}) %collective-permute-start) | collective-permute-done | bytes 131104 | tf_op jit(solution)/shard_map/ppermute | solution.py:198
  15.8 0.1 pad_maximum_fusion.refs_0_
  16.0 2.4 %collective-permute-start.4 = (bf16[8,16,1024]{2,1,0:T(8,128)(2,1)S(1)}, bf16[8,16,1024]{2,1,0:T(8,128)(2,1)S(1)}, u32[]{:S(2)}, u32[]{:S(2)}) collective-permute-start(bf16[8,16,1024]{2,1,0:T(8,128)(2,1)S(1)} %get-tuple-element.27), channel_id=1, source_target_pairs={{4,0},{8,4},{12,8},{16,12},{20,16},{24,20},{28,24},{5,1},{9,5},{13... | collective-permute-start | bytes 786440 | tf_op jit(solution)/shard_map/ppermute | solution.py:213
  18.4 4.1 %collective-permute-start.3 = (bf16[8,16,1024]{2,1,0:T(8,128)(2,1)S(1)}, bf16[8,16,1024]{2,1,0:T(8,128)(2,1)S(1)}, u32[]{:S(2)}, u32[]{:S(2)}) collective-permute-start(bf16[8,16,1024]{2,1,0:T(8,128)(2,1)S(1)} %get-tuple-element.28), channel_id=1, source_target_pairs={{0,4},{4,8},{8,12},{12,16},{16,20},{20,24},{24,28},{1,5},{5,9},{9,... | collective-permute-start | bytes 786440 | tf_op jit(solution)/shard_map/ppermute | solution.py:212
  22.4 0.0 copy-done.5
  22.4 0.0 copy-done.4
  22.5 0.0 copy-done.3
  22.5 1.1 %shard_map.64 = (bf16[512,512]{1,0:T(8,128)(2,1)S(1)}, bf16[512,512]{1,0:T(8,128)(2,1)S(1)}, bf16[8,512,256]{2,1,0:T(8,128)(2,1)S(1)}, bf16[8,512,256]{2,1,0:T(8,128)(2,1)S(1)}) custom-call(s32[1]{0:T(128)} %bitcast.2.depth_ref, f32[8,31]{1,0:T(8,128)S(1)} %copy-done.3, f32[8,31]{1,0:T(8,128)S(1)} %copy-done.4, f32[8,31]{1,0:T(8,128)S(1)} %copy-done.5), custom_call_target="tpu_custom_call" | custom-call | flops 100000000 | bytes 5242880 | tf_op jit(solution)/shard_map/pallas_call | solution.py:205
  23.5 1.8 %collective-permute-done.4.refs_2_ = bf16[8,16,1024]{2,1,0:T(8,128)(2,1)S(1)} collective-permute-done((bf16[8,16,1024]{2,1,0:T(8,128)(2,1)S(1)}, bf16[8,16,1024]{2,1,0:T(8,128)(2,1)S(1)}, u32[]{:S(2)}, u32[]{:S(2)}) %collective-permute-start.4) | collective-permute-done | bytes 262176 | tf_op jit(solution)/shard_map/ppermute | solution.py:213
  25.4 0.4 collective-permute-done.3.refs_1_
  25.7 0.0 copy-done.1
  25.7 0.0 copy-done.2
  25.7 0.0 copy-start
  25.7 3.9 %shard_map.65 = (f32[8,32,1024]{2,1,0:T(8,128)S(1)}, bf16[8,16,1024]{2,1,0:T(8,128)(2,1)S(1)}, bf16[8,16,1024]{2,1,0:T(8,128)(2,1)S(1)}) custom-call(s32[1]{0:T(128)} %bitcast.place_ref, s32[8]{0:T(128)S(1)} %copy-done.1, bf16[8,32,1024]{2,1,0:T(8,128)(2,1)S(1)} %pad_maximum_fusion.refs_0_, bf16[8,16,1024]{2,1,0:T(8,128)(2,1)S(1)} %collective-permute-done.3.refs_1_, ...), custom_call_target="tpu_custom_call" | custom-call | flops 2000000000 | bytes 10485760 | tf_op jit(solution)/shard_map/pallas_call | solution.py:215
  29.6 5.3 %collective-permute-start.5 = (bf16[8,16,1024]{2,1,0:T(8,128)(2,1)S(1)}, bf16[8,16,1024]{2,1,0:T(8,128)(2,1)S(1)}, u32[]{:S(2)}, u32[]{:S(2)}) collective-permute-start(bf16[8,16,1024]{2,1,0:T(8,128)(2,1)S(1)} %get-tuple-element.21), channel_id=1, source_target_pairs={{0,4},{4,8},{8,12},{12,16},{16,20},{20,24},{24,28},{1,5},{5,9},{9,... | collective-permute-start | bytes 786440 | tf_op jit(solution)/shard_map/ppermute | solution.py:228
  34.9 1.9 %collective-permute-start.6 = (bf16[8,16,1024]{2,1,0:T(8,128)(2,1)S(1)}, bf16[8,16,1024]{2,1,0:T(8,128)(2,1)S(1)}, u32[]{:S(2)}, u32[]{:S(2)}) collective-permute-start(bf16[8,16,1024]{2,1,0:T(8,128)(2,1)S(1)} %get-tuple-element.22), channel_id=1, source_target_pairs={{4,0},{8,4},{12,8},{16,12},{20,16},{24,20},{28,24},{5,1},{9,5},{13... | collective-permute-start | bytes 786440 | tf_op jit(solution)/shard_map/ppermute | solution.py:227
  36.9 3.2 %collective-permute-done.5.above_ref = bf16[8,16,1024]{2,1,0:T(8,128)(2,1)S(1)} collective-permute-done((bf16[8,16,1024]{2,1,0:T(8,128)(2,1)S(1)}, bf16[8,16,1024]{2,1,0:T(8,128)(2,1)S(1)}, u32[]{:S(2)}, u32[]{:S(2)}) %collective-permute-start.5) | collective-permute-done | bytes 262176 | tf_op jit(solution)/shard_map/ppermute | solution.py:228
  40.1 3.4 %collective-permute-done.6.below_ref = bf16[8,16,1024]{2,1,0:T(8,128)(2,1)S(1)} collective-permute-done((bf16[8,16,1024]{2,1,0:T(8,128)(2,1)S(1)}, bf16[8,16,1024]{2,1,0:T(8,128)(2,1)S(1)}, u32[]{:S(2)}, u32[]{:S(2)}) %collective-permute-start.6) | collective-permute-done | bytes 262176 | tf_op jit(solution)/shard_map/ppermute | solution.py:227
  43.5 0.2 shard_map.66
  43.7 0.1 collective-permute-start.7
  43.8 0.4 collective-permute-start.8
  44.2 1.3 %collective-permute-start.9 = (bf16[2,32,1024]{2,1,0:T(8,128)(2,1)S(1)}, bf16[2,32,1024]{2,1,0:T(8,128)(2,1)S(1)}, u32[]{:S(2)}, u32[]{:S(2)}) collective-permute-start(bf16[2,32,1024]{2,1,0:T(8,128)(2,1)S(1)} %get-tuple-element.26), channel_id=1, source_target_pairs={{0,3},{1,0},{2,1},{3,2},{4,7},{5,4},{6,5},{7,6},{8,11},{9,8},{10,9... | collective-permute-start | bytes 393224 | tf_op jit(solution)/shard_map/ppermute | solution.py:198
  45.5 3.5 %collective-permute-done.7.refs_0_ = bf16[2,32,1024]{2,1,0:T(8,128)(2,1)S(1)} collective-permute-done((bf16[2,32,1024]{2,1,0:T(8,128)(2,1)S(1)}, bf16[2,32,1024]{2,1,0:T(8,128)(2,1)S(1)}, u32[]{:S(2)}, u32[]{:S(2)}) %collective-permute-start.7) | collective-permute-done | bytes 131104 | tf_op jit(solution)/shard_map/ppermute | solution.py:198
  49.0 4.6 %collective-permute-done.8.refs_1_ = bf16[2,32,1024]{2,1,0:T(8,128)(2,1)S(1)} collective-permute-done((bf16[2,32,1024]{2,1,0:T(8,128)(2,1)S(1)}, bf16[2,32,1024]{2,1,0:T(8,128)(2,1)S(1)}, u32[]{:S(2)}, u32[]{:S(2)}) %collective-permute-start.8) | collective-permute-done | bytes 131104 | tf_op jit(solution)/shard_map/ppermute | solution.py:198
  53.6 1.6 %collective-permute-done.9.refs_2_ = bf16[2,32,1024]{2,1,0:T(8,128)(2,1)S(1)} collective-permute-done((bf16[2,32,1024]{2,1,0:T(8,128)(2,1)S(1)}, bf16[2,32,1024]{2,1,0:T(8,128)(2,1)S(1)}, u32[]{:S(2)}, u32[]{:S(2)}) %collective-permute-start.9) | collective-permute-done | bytes 131104 | tf_op jit(solution)/shard_map/ppermute | solution.py:198
  55.2 0.0 copy-done
  55.2 1.4 %shard_map.67 = f32[2,32,1024]{2,1,0:T(8,128)} custom-call(s32[1]{0:T(128)} %bitcast.place_ref, s32[8]{0:T(128)S(1)} %copy-done.1, f32[2,32,1024]{2,1,0:T(8,128)S(1)} %copy-done, f32[2,32,1024]{2,1,0:T(8,128)S(1)} %get-tuple-element.23.own_ref, bf16[2,32,1024]{2,1,0:T(8,128)(2,1)S(1)} %collective-permute-done.7.refs_0_, ...), custom_call_target="tpu_custom_call" | custom-call | flops 1000000 | bytes 1048576 | tf_op jit(solution)/shard_map/pallas_call | solution.py:236
  (1 shorter events, 0.0 us)
Async XLA Ops:
  0.0 22.4 %copy-start.5 = (f32[8,31]{1,0:T(8,128)S(1)}, f32[8,31]{1,0:T(8,128)}, u32[]{:S(2)}) copy-start(f32[8,31]{1,0:T(8,128)} %kz_ref.1) | copy-start | bytes 2980
  0.0 22.4 %copy-start.4 = (f32[8,31]{1,0:T(8,128)S(1)}, f32[8,31]{1,0:T(8,128)}, u32[]{:S(2)}) copy-start(f32[8,31]{1,0:T(8,128)} %ky_ref.1) | copy-start | bytes 2980
  0.0 22.5 %copy-start.3 = (f32[8,31]{1,0:T(8,128)S(1)}, f32[8,31]{1,0:T(8,128)}, u32[]{:S(2)}) copy-start(f32[8,31]{1,0:T(8,128)} %kx_ref.1) | copy-start | bytes 2980
  0.0 25.7 %copy-start.1 = (s32[8]{0:T(128)S(1)}, s32[8]{0:T(128)}, u32[]{:S(2)}) copy-start(s32[8]{0:T(128)} %offsets_ref.3) | copy-start | bytes 100
  0.0 25.7 %copy-start.2 = (bf16[8,2,32,1024]{3,2,1,0:T(8,128)(2,1)S(1)}, bf16[8,2,32,1024]{3,2,1,0:T(8,128)(2,1)}, u32[]{:S(2)}) copy-start(bf16[8,2,32,1024]{3,2,1,0:T(8,128)(2,1)} %param.7) | copy-start | bytes 3145732
  1.1 4.4 %collective-permute-start.2 = (bf16[2,32,1024]{2,1,0:T(8,128)(2,1)S(1)}, bf16[2,32,1024]{2,1,0:T(8,128)(2,1)S(1)}, u32[]{:S(2)}, u32[]{:S(2)}) collective-permute-start(bf16[2,32,1024]{2,1,0:T(8,128)(2,1)S(1)} %convert_element_type.3), channel_id=1, source_target_pairs={{0,1},{1,2},{2,3},{3,0},{4,5},{5,6},{6,7},{7,4},{8,9},{9,10},{10,1... | collective-permute-start | bytes 393224 | tf_op jit(solution)/shard_map/ppermute | solution.py:198
  2.4 10.6 %collective-permute-start.1 = (bf16[2,32,1024]{2,1,0:T(8,128)(2,1)S(1)}, bf16[2,32,1024]{2,1,0:T(8,128)(2,1)S(1)}, u32[]{:S(2)}, u32[]{:S(2)}) collective-permute-start(bf16[2,32,1024]{2,1,0:T(8,128)(2,1)S(1)} %convert_element_type.3), channel_id=1, source_target_pairs={{0,2},{1,3},{2,0},{3,1},{4,6},{5,7},{6,4},{7,5},{8,10},{9,11},{10,... | collective-permute-start | bytes 393224 | tf_op jit(solution)/shard_map/ppermute | solution.py:198
  3.5 12.3 %collective-permute-start = (bf16[2,32,1024]{2,1,0:T(8,128)(2,1)S(1)}, bf16[2,32,1024]{2,1,0:T(8,128)(2,1)S(1)}, u32[]{:S(2)}, u32[]{:S(2)}) collective-permute-start(bf16[2,32,1024]{2,1,0:T(8,128)(2,1)S(1)} %convert_element_type.3), channel_id=1, source_target_pairs={{0,3},{1,0},{2,1},{3,2},{4,7},{5,4},{6,5},{7,6},{8,11},{9,8},{10,9... | collective-permute-start | bytes 393224 | tf_op jit(solution)/shard_map/ppermute | solution.py:198
  16.0 9.4 %collective-permute-start.4 = (bf16[8,16,1024]{2,1,0:T(8,128)(2,1)S(1)}, bf16[8,16,1024]{2,1,0:T(8,128)(2,1)S(1)}, u32[]{:S(2)}, u32[]{:S(2)}) collective-permute-start(bf16[8,16,1024]{2,1,0:T(8,128)(2,1)S(1)} %get-tuple-element.27), channel_id=1, source_target_pairs={{4,0},{8,4},{12,8},{16,12},{20,16},{24,20},{28,24},{5,1},{9,5},{13... | collective-permute-start | bytes 786440 | tf_op jit(solution)/shard_map/ppermute | solution.py:213
  18.4 7.4 %collective-permute-start.3 = (bf16[8,16,1024]{2,1,0:T(8,128)(2,1)S(1)}, bf16[8,16,1024]{2,1,0:T(8,128)(2,1)S(1)}, u32[]{:S(2)}, u32[]{:S(2)}) collective-permute-start(bf16[8,16,1024]{2,1,0:T(8,128)(2,1)S(1)} %get-tuple-element.28), channel_id=1, source_target_pairs={{0,4},{4,8},{8,12},{12,16},{16,20},{20,24},{24,28},{1,5},{5,9},{9,... | collective-permute-start | bytes 786440 | tf_op jit(solution)/shard_map/ppermute | solution.py:212
  25.7 29.5 %copy-start = (f32[2,32,1024]{2,1,0:T(8,128)S(1)}, f32[2,32,1024]{2,1,0:T(8,128)}, u32[]{:S(2)}) copy-start(f32[2,32,1024]{2,1,0:T(8,128)} %estimate_ref.1) | copy-start | bytes 786436
  29.6 10.5 %collective-permute-start.5 = (bf16[8,16,1024]{2,1,0:T(8,128)(2,1)S(1)}, bf16[8,16,1024]{2,1,0:T(8,128)(2,1)S(1)}, u32[]{:S(2)}, u32[]{:S(2)}) collective-permute-start(bf16[8,16,1024]{2,1,0:T(8,128)(2,1)S(1)} %get-tuple-element.21), channel_id=1, source_target_pairs={{0,4},{4,8},{8,12},{12,16},{16,20},{20,24},{24,28},{1,5},{5,9},{9,... | collective-permute-start | bytes 786440 | tf_op jit(solution)/shard_map/ppermute | solution.py:228
  34.9 8.6 %collective-permute-start.6 = (bf16[8,16,1024]{2,1,0:T(8,128)(2,1)S(1)}, bf16[8,16,1024]{2,1,0:T(8,128)(2,1)S(1)}, u32[]{:S(2)}, u32[]{:S(2)}) collective-permute-start(bf16[8,16,1024]{2,1,0:T(8,128)(2,1)S(1)} %get-tuple-element.22), channel_id=1, source_target_pairs={{4,0},{8,4},{12,8},{16,12},{20,16},{24,20},{28,24},{5,1},{9,5},{13... | collective-permute-start | bytes 786440 | tf_op jit(solution)/shard_map/ppermute | solution.py:227
  43.7 5.3 %collective-permute-start.7 = (bf16[2,32,1024]{2,1,0:T(8,128)(2,1)S(1)}, bf16[2,32,1024]{2,1,0:T(8,128)(2,1)S(1)}, u32[]{:S(2)}, u32[]{:S(2)}) collective-permute-start(bf16[2,32,1024]{2,1,0:T(8,128)(2,1)S(1)} %get-tuple-element.24), channel_id=1, source_target_pairs={{0,1},{1,2},{2,3},{3,0},{4,5},{5,6},{6,7},{7,4},{8,9},{9,10},{10,1... | collective-permute-start | bytes 393224 | tf_op jit(solution)/shard_map/ppermute | solution.py:198
  43.8 9.8 %collective-permute-start.8 = (bf16[2,32,1024]{2,1,0:T(8,128)(2,1)S(1)}, bf16[2,32,1024]{2,1,0:T(8,128)(2,1)S(1)}, u32[]{:S(2)}, u32[]{:S(2)}) collective-permute-start(bf16[2,32,1024]{2,1,0:T(8,128)(2,1)S(1)} %get-tuple-element.25), channel_id=1, source_target_pairs={{0,2},{1,3},{2,0},{3,1},{4,6},{5,7},{6,4},{7,5},{8,10},{9,11},{10,... | collective-permute-start | bytes 393224 | tf_op jit(solution)/shard_map/ppermute | solution.py:198
  44.2 11.0 %collective-permute-start.9 = (bf16[2,32,1024]{2,1,0:T(8,128)(2,1)S(1)}, bf16[2,32,1024]{2,1,0:T(8,128)(2,1)S(1)}, u32[]{:S(2)}, u32[]{:S(2)}) collective-permute-start(bf16[2,32,1024]{2,1,0:T(8,128)(2,1)S(1)} %get-tuple-element.26), channel_id=1, source_target_pairs={{0,3},{1,0},{2,1},{3,2},{4,7},{5,4},{6,5},{7,6},{8,11},{9,8},{10,9... | collective-permute-start | bytes 393224 | tf_op jit(solution)/shard_map/ppermute | solution.py:198

commit v2 on v1

--- a/solution.py
+++ b/solution.py
@@ -29,11 +29,10 @@
     return pltpu.roll(spread, 0, 1, stride=1, stride_axis=0)
 
 
-def matrices_kernel(planes, strip, depth_ref, kx_ref, ky_ref, kz_ref, w_ref, wt_ref, tf_ref, tb_ref):
+def matrices_kernel(planes, strip, device_ref, kx_ref, ky_ref, kz_ref, w_ref, wt_ref, tf_ref, tb_ref):
     views, taps = kx_ref.shape
     margin = taps // 2
     extent = strip + 2 * HALO
-    depth = w_ref.shape[1] // (planes * extent)
     kx, ky, kz = normalized(kx_ref), normalized(ky_ref), normalized(kz_ref)
     lane = lax.broadcasted_iota(jnp.int32, (1, LANES), 1)
     x_row = select_taps(lane % extent - (HALO - margin), kx)
@@ -41,13 +40,20 @@
     forward_row = select_taps(margin - near, ky)
     backward_row = select_taps(margin + near, ky)
     column = lax.broadcasted_iota(jnp.int32, (1, w_ref.shape[1]), 1) // extent
-    device = depth_ref[0]
-    source = device + column // planes
-    source = jnp.where(source >= depth, source - depth, source)
-    plane = source * planes + column % planes
+    device, odd = device_ref[0], device_ref[1] == 1
+    plane = (device ^ (column // planes)) * planes + column % planes
+    spot = lax.broadcasted_iota(jnp.int32, (strip, LANES), 1) % extent
+    swap_first = jnp.logical_and(spot < HALO, jnp.logical_not(odd))
+    swap_last = jnp.logical_and(spot >= extent - HALO, jnp.logical_not(odd))
     z_rows = [select_taps(plane - (device * planes + own) + margin, kz) for own in range(planes)]
     for view in range(views):
         x_block = slanted(x_row[view : view + 1], strip)
+        turn = extent - HALO
+        x_block = jnp.where(
+            swap_first,
+            pltpu.roll(x_block, LANES - turn, 1),
+            jnp.where(swap_last, pltpu.roll(x_block, turn, 1), x_block),
+        )
         x_block = jnp.concatenate([x_block] * (w_ref.shape[1] // LANES), axis=1)
         for own in range(planes):
             first = (view * planes + own) * strip
@@ -87,18 +93,19 @@
     return base + values[..., first : first + LANES].astype(F32)
 
 
-def main_kernel(planes, strip, view_rows, place_ref, offsets_ref, *refs):
-    (all_ref, before_ref, after_ref, views_ref, w_ref, wt_ref, tf_ref, tb_ref,
-     core_ref, top_ref, bottom_ref, ext_ref, pad_ref, back_ref, deep_ref) = refs
+def main_kernel(planes, strip, view_rows, depth, place_ref, offsets_ref, *refs):
+    chunks, outer, refs = refs[:depth], refs[depth : 2 * depth], refs[2 * depth :]
+    inner_ref, views_ref, w_ref, wt_ref, tf_ref, tb_ref, core_ref, back1_ref = refs[:8]
+    back2, (ext_ref, pad_ref, back_ref, deep_ref) = refs[8:-4], refs[-4:]
     views = offsets_ref.shape[0]
     extent = strip + 2 * HALO
-    columns = all_ref.shape[-1]
+    columns = ext_ref.shape[-1]
     group = planes * strip
-    for p in range(all_ref.shape[0]):
+    for p in range(depth * planes):
         first = p * extent
-        ext_ref[first : first + HALO, :] = before_ref[p]
-        ext_ref[first + HALO : first + HALO + strip, :] = all_ref[p]
-        ext_ref[first + HALO + strip : first + extent, :] = after_ref[p]
+        ext_ref[first : first + HALO, :] = inner_ref[p]
+        ext_ref[first + HALO : first + HALO + strip, :] = chunks[p // planes][p % planes]
+        ext_ref[first + HALO + strip : first + extent, :] = outer[p // planes][p % planes]
     for pad in (pad_ref, back_ref):
         pad[:, :LANES] = jnp.zeros((pad.shape[0], LANES), BF16)
         pad[:, LANES + columns :] = jnp.zeros((pad.shape[0], LANES), BF16)
@@ -126,23 +133,25 @@
             deep_ref[rows, first : first + WIDE] = backward[n * group : (n + 1) * group].astype(BF16)
     for p in range(core_ref.shape[0]):
         part = jnp.dot(wt_ref[p * extent : (p + 1) * extent], deep_ref[...], preferred_element_type=F32)
-        core_ref[p] = part[HALO : HALO + strip]
-        write_coded(top_ref, (p, slice(None)), part[:HALO])
-        write_coded(bottom_ref, (p, slice(None)), part[HALO + strip :])
-
-
-def join_kernel(planes, core_ref, above_ref, below_ref, own_ref, *sends):
+        core_ref[p] = part[HALO : extent - HALO]
+        write_coded(back1_ref, (p, slice(None)), part[:HALO])
+        write_coded(back2[p // planes], (p % planes, slice(None)), part[extent - HALO :])
+
+
+def join_kernel(planes, device_ref, core_ref, inner_ref, own_ref, *sends):
     strip = core_ref.shape[1]
     columns = core_ref.shape[2]
+    odd = device_ref[1] == 1
     for p in range(core_ref.shape[0]):
-        above, below = above_ref[p], below_ref[p]
+        inner = inner_ref[p]
         parts = []
         for first in range(0, columns, LANES):
             lanes = slice(first, first + LANES)
-            tail = core_ref[p, strip - HALO :, lanes] + decoded(below, first)
-            head = core_ref[p, :HALO, lanes] + decoded(above, first)
-            inner = [core_ref[p, HALO : strip - HALO, lanes]] if strip > 2 * HALO else []
-            parts.append(jnp.concatenate([head, *inner, tail], axis=0))
+            added = decoded(inner, first)
+            head = core_ref[p, :HALO, lanes] + jnp.where(odd, added, 0.0)
+            tail = core_ref[p, strip - HALO :, lanes] + jnp.where(odd, 0.0, added)
+            middle = [core_ref[p, HALO : strip - HALO, lanes]] if strip > 2 * HALO else []
+            parts.append(jnp.concatenate([head, *middle, tail], axis=0))
         whole = jnp.concatenate(parts, axis=1)
         if p < planes:
             own_ref[p] = whole
@@ -150,9 +159,12 @@
             write_coded(sends[p // planes - 1], (p % planes, slice(None)), whole)
 
 
-def update_kernel(view_rows, place_ref, offsets_ref, estimate_ref, own_ref, *refs):
+def update_kernel(view_rows, place_ref, device_ref, offsets_ref, estimate_ref, own_ref, *refs):
     received, out_ref = refs[:-1], refs[-1]
+    near = len(received) // 2
+    received, outer = received[:near], received[near:]
     planes, strip, columns = estimate_ref.shape
+    odd = device_ref[1] == 1
     row = place_ref[0] + lax.broadcasted_iota(jnp.int32, (strip, LANES), 0)
     coverage = jnp.zeros((strip, LANES), F32)
     for view in range(offsets_ref.shape[0]):
@@ -165,6 +177,13 @@
             summed = own_ref[p, :, lanes]
             for ref in received:
                 summed = summed + decoded(ref[p], first)
+            edge = decoded(outer[0][p], first)
+            for ref in outer[1:]:
+                edge = edge + decoded(ref[p], first)
+            head = summed[:HALO] + jnp.where(odd, 0.0, edge)
+            tail = summed[strip - HALO :] + jnp.where(odd, edge, 0.0)
+            middle = [summed[HALO : strip - HALO]] if strip > 2 * HALO else []
+            summed = jnp.concatenate([head, *middle, tail], axis=0)
             out_ref[p, :, lanes] = estimate_ref[p, :, lanes] * (1.0 + summed * scale)
 
 
@@ -188,34 +207,46 @@
     count = views.shape[0]
     extent = strip + 2 * HALO
     rows = count * planes * strip
-    deep = depth * planes
-    inner = deep * extent
+    inner = depth * planes * extent
     view_rows = 5 * strip * tiles // 8
-    place = (lax.axis_index("tile") * strip).astype(jnp.int32).reshape(1)
-    device = lax.axis_index("depth").astype(jnp.int32).reshape(1)
-
-    def turned(array, shift):
-        return lax.ppermute(array, "depth", [(i, (i - shift) % depth) for i in range(depth)])
-
-    up = [(i, i + 1) for i in range(tiles - 1)]
-    down = [(j, i) for i, j in up]
+    tile = lax.axis_index("tile").astype(jnp.int32)
+    odd = tile % 2
+    place = (tile * strip).reshape(1)
+    device = jnp.stack([lax.axis_index("depth").astype(jnp.int32), odd])
+    steps = range(depth)
+
+    def across(array, step):
+        return lax.ppermute(array, "depth", [(i, i ^ step) for i in range(depth)])
+
+    def beside(array, step):
+        pairs = [(i, i - 1 + 2 * (i % 2)) for i in range(1, tiles - 1)]
+        pairs = [(i * depth + d, j * depth + (d ^ step)) for i, j in pairs for d in range(depth)]
+        return lax.ppermute(array, ("tile", "depth"), pairs)
+
+    def within(array):
+        return lax.ppermute(array, "tile", [(i, i ^ 1) for i in range(tiles)])
+
+    def early_or_late(array, early):
+        return jnp.where(odd == early, array[:, :HALO], array[:, strip - HALO :])
 
     own = estimate.astype(BF16)
-    chunks = [own] + [turned(own, shift) for shift in range(1, depth)]
+    edge = early_or_late(own, 0)
+    chunks = [own] + [across(own, step) for step in steps[1:]]
+    outer = [beside(edge, step) for step in steps]
+    chunks, outer = lax.optimization_barrier((chunks, outer))
     w, wt, tf, tb = call(
         functools.partial(matrices_kernel, planes, strip),
         (shape((rows, inner), BF16), shape((inner, rows), BF16))
         + (shape((count, WIDE + 2 * LANES, WIDE), BF16),) * 2,
         1, 3, flops=10**8, moved=5 * 2**20,
     )(device, kernel_x, kernel_y, kernel_z)
-    gathered = jnp.concatenate(chunks, axis=0)
-    before = lax.ppermute(gathered[:, strip - HALO :], "tile", up)
-    after = lax.ppermute(gathered[:, :HALO], "tile", down)
-    halo = shape((deep, HALO, columns), BF16)
-    core, top, bottom = call(
-        functools.partial(main_kernel, planes, strip, view_rows),
-        (shape((deep, strip, columns), F32), halo, halo),
-        2, 8,
+    inside = within(early_or_late(jnp.concatenate(chunks, axis=0), 1))
+    halo = shape((planes, HALO, columns), BF16)
+    core, back1, *back2 = call(
+        functools.partial(main_kernel, planes, strip, view_rows, depth),
+        (shape((depth * planes, strip, columns), F32), shape((depth * planes, HALO, columns), BF16))
+        + (halo,) * depth,
+        2, 2 * depth + 6,
         scratch=(
             pltpu.VMEM((inner, columns), BF16),
             pltpu.VMEM((rows, columns + 2 * LANES), BF16),
@@ -223,21 +254,20 @@
             pltpu.VMEM((rows, columns), BF16),
         ),
         flops=2 * 10**9, moved=10 * 2**20,
-    )(place, offsets, gathered, before, after, views.reshape(rows, columns), w, wt, tf, tb)
-    below = lax.ppermute(top, "tile", down)
-    above = lax.ppermute(bottom, "tile", up)
+    )(place, offsets, *chunks, *outer, inside, views.reshape(rows, columns), w, wt, tf, tb)
     block = (planes, strip, columns)
     own_sum, *sends = call(
         functools.partial(join_kernel, planes),
         (shape(block, F32),) + (shape(block, BF16),) * (depth - 1),
-        0, 3, flops=10**6, moved=3 * 2**20,
-    )(core, above, below)
-    received = [turned(send, depth - 1 - n) for n, send in enumerate(sends)]
+        1, 2, flops=10**6, moved=3 * 2**20,
+    )(device, core, within(back1))
+    received = [across(send, step) for send, step in zip(sends, steps[1:])]
+    edges = [beside(send, step) for send, step in zip(back2, steps)]
     return call(
         functools.partial(update_kernel, view_rows),
         shape(block, F32),
-        2, 2 + len(received), flops=10**6, moved=2**20,
-    )(place, offsets, estimate, own_sum, *received)
+        3, 1 + 2 * depth, flops=10**6, moved=2**20,
+    )(place, device, offsets, estimate, own_sum, *received, *edges[::-1])
 
 
 def solution(mesh):

time: 56.8 us -> 60.9 us (1.072)
  starting transfers between devices: 19.3 us -> 42.5 us
  waiting for transfers between devices: 29.5 us -> 8.86 us
  Pallas kernels: 6.52 us -> 7.72 us
    ppermute x10 -> x16, starting transfers between devices: 19.3 us -> 42.5 us  [the longest x8 35.5 us: beside(): return lax.ppermute(array, ('tile', 'depth'), pairs)]
    ppermute x10 -> x16, waiting for transfers between devices: 29.5 us -> 8.86 us  [the longest x8 7.65 us: beside(): return lax.ppermute(array, ('tile', 'depth'), pairs)]
  transfers between devices with their start and end apart: 10 -> 16, of which waited for: 10 -> 6; matrix products, arithmetic and copies ran while one was open for 0% -> 0% of each run, Pallas kernels for 2% -> 4%
where the time goes in v2:
time: 60.9 us; the launch traced here: 60.6 us
  starting transfers between devices  42.5 us (70%)
  waiting for transfers between devices  8.86 us (15%)
  Pallas kernels  7.72 us (13%)
  other arithmetic  1.18 us (2%)
    ppermute x8, starting transfers between devices, beside(): return lax.ppermute(array, ('tile', 'depth'), pairs)  35.5 us
    ppermute x8, waiting for transfers between devices, beside(): return lax.ppermute(array, ('tile', 'depth'), pairs)  7.65 us
    ppermute x6, starting transfers between devices, across(): return lax.ppermute(array, 'depth', [(i, i ^ step) for i in range(depth)])  6.45 us
    pallas_call x1, Pallas kernels, shards(): call(functools.partial(main_kernel, planes, strip, view_rows, depth), (sh...  3.92 us
    pallas_call x1, Pallas kernels, shards(): call(functools.partial(matrices_kernel, planes, strip), (shape((rows, inn...  1.65 us
    pallas_call x1, Pallas kernels, shards(): call(functools.partial(update_kernel, view_rows), shape(block, F32), 3, 1...  1.45 us
  transfers between devices with their start and end apart: 16, of which 6 were waited for; matrix products, arithmetic and copies ran while one was open for 0% of the time, Pallas kernels for 4%

profile of v2, /device:TPU:11, one launch (start us, length us, event | category | flops | bytes accessed | tf_op | source)
XLA Modules:
  0.0 60.6 jit_solution(11777561592439325191)
XLA Ops:
  0.0 0.0 copy-start.5
  0.0 0.0 copy-start.4
  0.0 0.0 copy-start.3
  0.0 0.0 copy-start.1
  0.0 0.0 copy-start.2
  0.0 1.1 %convert_element_type.3.refs_0_ = bf16[2,32,1024]{2,1,0:T(8,128)(2,1)S(1)} convert(f32[2,32,1024]{2,1,0:T(8,128)} %estimate_ref.1) | non-fusion elementwise | flops 65536 | bytes 393216 | tf_op jit(solution)/shard_map/convert_element_type | solution.py:232
  1.1 4.7 %collective-permute-start.6 = (bf16[2,16,1024]{2,1,0:T(8,128)(2,1)S(1)}, bf16[2,16,1024]{2,1,0:T(8,128)(2,1)S(1)}, u32[]{:S(2)}, u32[]{:S(2)}) collective-permute-start(bf16[2,16,1024]{2,1,0:T(8,128)(2,1)S(1)} %slice_select_fusion.1), channel_id=1, source_target_pairs={{4,11},{5,10},{6,9},{7,8},{8,7},{9,6},{10,5},{11,4},{12,19},{13,18... | collective-permute-start | bytes 196616 | tf_op jit(solution)/shard_map/ppermute | solution.py:224
  5.8 3.5 %collective-permute-start.5 = (bf16[2,16,1024]{2,1,0:T(8,128)(2,1)S(1)}, bf16[2,16,1024]{2,1,0:T(8,128)(2,1)S(1)}, u32[]{:S(2)}, u32[]{:S(2)}) collective-permute-start(bf16[2,16,1024]{2,1,0:T(8,128)(2,1)S(1)} %slice_select_fusion.1), channel_id=1, source_target_pairs={{4,10},{5,11},{6,8},{7,9},{8,6},{9,7},{10,4},{11,5},{12,18},{13,19... | collective-permute-start | bytes 196616 | tf_op jit(solution)/shard_map/ppermute | solution.py:224
  9.3 2.5 %collective-permute-start.2 = (bf16[2,32,1024]{2,1,0:T(8,128)(2,1)S(1)}, bf16[2,32,1024]{2,1,0:T(8,128)(2,1)S(1)}, u32[]{:S(2)}, u32[]{:S(2)}) collective-permute-start(bf16[2,32,1024]{2,1,0:T(8,128)(2,1)S(1)} %convert_element_type.3.refs_0_), channel_id=1, source_target_pairs={{0,3},{1,2},{2,1},{3,0},{4,7},{5,6},{6,5},{7,4},{8,11},{9,10},{10,... | collective-permute-start | bytes 393224 | tf_op jit(solution)/shard_map/ppermute | solution.py:219
  11.8 0.3 collective-permute-start.1
  12.1 0.9 %collective-permute-start = (bf16[2,32,1024]{2,1,0:T(8,128)(2,1)S(1)}, bf16[2,32,1024]{2,1,0:T(8,128)(2,1)S(1)}, u32[]{:S(2)}, u32[]{:S(2)}) collective-permute-start(bf16[2,32,1024]{2,1,0:T(8,128)(2,1)S(1)} %convert_element_type.3.refs_0_), channel_id=1, source_target_pairs={{0,1},{1,0},{2,3},{3,2},{4,5},{5,4},{6,7},{7,6},{8,9},{9,8},{10,11... | collective-permute-start | bytes 393224 | tf_op jit(solution)/shard_map/ppermute | solution.py:219
  13.0 0.0 collective-permute-done.6.refs_7_
  13.0 4.5 %collective-permute-start.4 = (bf16[2,16,1024]{2,1,0:T(8,128)(2,1)S(1)}, bf16[2,16,1024]{2,1,0:T(8,128)(2,1)S(1)}, u32[]{:S(2)}, u32[]{:S(2)}) collective-permute-start(bf16[2,16,1024]{2,1,0:T(8,128)(2,1)S(1)} %slice_select_fusion.1), channel_id=1, source_target_pairs={{4,9},{5,8},{6,11},{7,10},{8,5},{9,4},{10,7},{11,6},{12,17},{13,16... | collective-permute-start | bytes 196616 | tf_op jit(solution)/shard_map/ppermute | solution.py:224
  17.5 0.6 collective-permute-done.5.refs_6_
  18.1 3.3 %collective-permute-start.3 = (bf16[2,16,1024]{2,1,0:T(8,128)(2,1)S(1)}, bf16[2,16,1024]{2,1,0:T(8,128)(2,1)S(1)}, u32[]{:S(2)}, u32[]{:S(2)}) collective-permute-start(bf16[2,16,1024]{2,1,0:T(8,128)(2,1)S(1)} %slice_select_fusion.1), channel_id=1, source_target_pairs={{4,8},{5,9},{6,10},{7,11},{8,4},{9,5},{10,6},{11,7},{12,16},{13,17... | collective-permute-start | bytes 196616 | tf_op jit(solution)/shard_map/ppermute | solution.py:224
  21.4 1.7 %collective-permute-done.4.refs_5_ = bf16[2,16,1024]{2,1,0:T(8,128)(2,1)S(1)} collective-permute-done((bf16[2,16,1024]{2,1,0:T(8,128)(2,1)S(1)}, bf16[2,16,1024]{2,1,0:T(8,128)(2,1)S(1)}, u32[]{:S(2)}, u32[]{:S(2)}) %collective-permute-start.4) | collective-permute-done | bytes 65568 | tf_op jit(solution)/shard_map/ppermute | solution.py:224
  23.1 1.5 %collective-permute-done.3.refs_4_ = bf16[2,16,1024]{2,1,0:T(8,128)(2,1)S(1)} collective-permute-done((bf16[2,16,1024]{2,1,0:T(8,128)(2,1)S(1)}, bf16[2,16,1024]{2,1,0:T(8,128)(2,1)S(1)}, u32[]{:S(2)}, u32[]{:S(2)}) %collective-permute-start.3) | collective-permute-done | bytes 65568 | tf_op jit(solution)/shard_map/ppermute | solution.py:224
  24.6 0.0 collective-permute-done.2.refs_3_
  24.6 0.0 collective-permute-done.1.refs_2_
  24.6 0.0 collective-permute-done.refs_1_
  24.7 0.1 collective-permute-start.7
  24.8 0.1 pad_add_fusion.device_ref
  24.9 0.0 copy-done.5
  24.9 0.0 copy-done.4
  24.9 0.0 copy-done.3
  24.9 1.7 %shard_map.64 = (bf16[512,512]{1,0:T(8,128)(2,1)S(1)}, bf16[512,512]{1,0:T(8,128)(2,1)S(1)}, bf16[8,512,256]{2,1,0:T(8,128)(2,1)S(1)}, bf16[8,512,256]{2,1,0:T(8,128)(2,1)S(1)}) custom-call(s32[2]{0:T(128)S(1)} %pad_add_fusion.device_ref, f32[8,31]{1,0:T(8,128)S(1)} %copy-done.3, f32[8,31]{1,0:T(8,128)S(1)} %copy-done.4, f32[8,31]{1,0:T(8,128)S(1)} %copy-done.5), custom_call_target="tpu_custom_call" | custom-call | flops 100000000 | bytes 5242880 | tf_op jit(solution)/shard_map/pallas_call | solution.py:237
  26.5 0.0 collective-permute-done.7.refs_8_
  26.5 0.0 copy-done.1
  26.5 0.0 copy-done.2
  26.6 0.0 copy-start
  26.6 3.9 %shard_map.65 = (f32[8,32,1024]{2,1,0:T(8,128)S(1)}, bf16[8,16,1024]{2,1,0:T(8,128)(2,1)S(1)}, bf16[2,16,1024]{2,1,0:T(8,128)(2,1)S(1)}, bf16[2,16,1024]{2,1,0:T...) custom-call(s32[1]{0:T(128)} %bitcast.place_ref, s32[8]{0:T(128)S(1)} %copy-done.1, ...), custom_call_target="tpu_custom_call" | custom-call | flops 2000000000 | bytes 10485760 | tf_op jit(solution)/shard_map/pallas_call | solution.py:245
  30.5 0.6 collective-permute-start.8
  31.0 4.9 %collective-permute-start.12 = (bf16[2,16,1024]{2,1,0:T(8,128)(2,1)S(1)}, bf16[2,16,1024]{2,1,0:T(8,128)(2,1)S(1)}, u32[]{:S(2)}, u32[]{:S(2)}) collective-permute-start(bf16[2,16,1024]{2,1,0:T(8,128)(2,1)S(1)} %get-tuple-element.45), channel_id=1, source_target_pairs={{4,11},{5,10},{6,9},{7,8},{8,7},{9,6},{10,5},{11,4},{12,19},{13,18... | collective-permute-start | bytes 196616 | tf_op jit(solution)/shard_map/ppermute | solution.py:224
  36.0 7.5 %collective-permute-start.13 = (bf16[2,16,1024]{2,1,0:T(8,128)(2,1)S(1)}, bf16[2,16,1024]{2,1,0:T(8,128)(2,1)S(1)}, u32[]{:S(2)}, u32[]{:S(2)}) collective-permute-start(bf16[2,16,1024]{2,1,0:T(8,128)(2,1)S(1)} %get-tuple-element.46), channel_id=1, source_target_pairs={{4,10},{5,11},{6,8},{7,9},{8,6},{9,7},{10,4},{11,5},{12,18},{13,19... | collective-permute-start | bytes 196616 | tf_op jit(solution)/shard_map/ppermute | solution.py:224
  43.5 0.0 collective-permute-done.8.inner_ref
  43.5 0.7 %shard_map.66 = (f32[2,32,1024]{2,1,0:T(8,128)S(1)}, bf16[2,32,1024]{2,1,0:T(8,128)(2,1)S(1)}, bf16[2,32,1024]{2,1,0:T(8,128)(2,1)S(1)}, bf16[2,32,1024]{2,1,0:T(8,128)(2,1)S(1)}) custom-call(s32[2]{0:T(128)S(1)} %pad_add_fusion.device_ref, f32[8,32,1024]{2,1,0:T(8,128)S(1)} %get-tuple-element.39.core_ref, ...), custom_call_target="tpu_custom_call" | custom-call | flops 1000000 | bytes 3145728 | tf_op jit(solution)/shard_map/pallas_call | solution.py:259
  44.2 0.1 collective-permute-start.9
  44.3 1.1 %collective-permute-start.10 = (bf16[2,32,1024]{2,1,0:T(8,128)(2,1)S(1)}, bf16[2,32,1024]{2,1,0:T(8,128)(2,1)S(1)}, u32[]{:S(2)}, u32[]{:S(2)}) collective-permute-start(bf16[2,32,1024]{2,1,0:T(8,128)(2,1)S(1)} %get-tuple-element.43), channel_id=1, source_target_pairs={{0,2},{1,3},{2,0},{3,1},{4,6},{5,7},{6,4},{7,5},{8,10},{9,11},{10,... | collective-permute-start | bytes 393224 | tf_op jit(solution)/shard_map/ppermute | solution.py:219
  45.4 1.6 %collective-permute-start.11 = (bf16[2,32,1024]{2,1,0:T(8,128)(2,1)S(1)}, bf16[2,32,1024]{2,1,0:T(8,128)(2,1)S(1)}, u32[]{:S(2)}, u32[]{:S(2)}) collective-permute-start(bf16[2,32,1024]{2,1,0:T(8,128)(2,1)S(1)} %get-tuple-element.44), channel_id=1, source_target_pairs={{0,3},{1,2},{2,1},{3,0},{4,7},{5,6},{6,5},{7,4},{8,11},{9,10},{10,... | collective-permute-start | bytes 393224 | tf_op jit(solution)/shard_map/ppermute | solution.py:219
  46.9 0.0 collective-permute-done.12.refs_3_
  46.9 4.5 %collective-permute-start.14 = (bf16[2,16,1024]{2,1,0:T(8,128)(2,1)S(1)}, bf16[2,16,1024]{2,1,0:T(8,128)(2,1)S(1)}, u32[]{:S(2)}, u32[]{:S(2)}) collective-permute-start(bf16[2,16,1024]{2,1,0:T(8,128)(2,1)S(1)} %get-tuple-element.47), channel_id=1, source_target_pairs={{4,9},{5,8},{6,11},{7,10},{8,5},{9,4},{10,7},{11,6},{12,17},{13,16... | collective-permute-start | bytes 196616 | tf_op jit(solution)/shard_map/ppermute | solution.py:224
  51.5 0.0 collective-permute-done.13.refs_4_
  51.5 2.6 %collective-permute-start.15 = (bf16[2,16,1024]{2,1,0:T(8,128)(2,1)S(1)}, bf16[2,16,1024]{2,1,0:T(8,128)(2,1)S(1)}, u32[]{:S(2)}, u32[]{:S(2)}) collective-permute-start(bf16[2,16,1024]{2,1,0:T(8,128)(2,1)S(1)} %get-tuple-element.48), channel_id=1, source_target_pairs={{4,8},{5,9},{6,10},{7,11},{8,4},{9,5},{10,6},{11,7},{12,16},{13,17... | collective-permute-start | bytes 196616 | tf_op jit(solution)/shard_map/ppermute | solution.py:224
  54.1 2.3 %collective-permute-done.14.refs_5_ = bf16[2,16,1024]{2,1,0:T(8,128)(2,1)S(1)} collective-permute-done((bf16[2,16,1024]{2,1,0:T(8,128)(2,1)S(1)}, bf16[2,16,1024]{2,1,0:T(8,128)(2,1)S(1)}, u32[]{:S(2)}, u32[]{:S(2)}) %collective-permute-start.14) | collective-permute-done | bytes 65568 | tf_op jit(solution)/shard_map/ppermute | solution.py:224
  56.4 1.6 %collective-permute-done.15.refs_6_ = bf16[2,16,1024]{2,1,0:T(8,128)(2,1)S(1)} collective-permute-done((bf16[2,16,1024]{2,1,0:T(8,128)(2,1)S(1)}, bf16[2,16,1024]{2,1,0:T(8,128)(2,1)S(1)}, u32[]{:S(2)}, u32[]{:S(2)}) %collective-permute-start.15) | collective-permute-done | bytes 65568 | tf_op jit(solution)/shard_map/ppermute | solution.py:224
  58.0 0.0 collective-permute-done.9.refs_0_
  58.0 0.0 collective-permute-done.10.refs_1_
  58.0 1.2 %collective-permute-done.11.refs_2_ = bf16[2,32,1024]{2,1,0:T(8,128)(2,1)S(1)} collective-permute-done((bf16[2,32,1024]{2,1,0:T(8,128)(2,1)S(1)}, bf16[2,32,1024]{2,1,0:T(8,128)(2,1)S(1)}, u32[]{:S(2)}, u32[]{:S(2)}) %collective-permute-start.11) | collective-permute-done | bytes 131104 | tf_op jit(solution)/shard_map/ppermute | solution.py:219
  59.2 0.0 copy-done
  59.2 1.5 %shard_map.67 = f32[2,32,1024]{2,1,0:T(8,128)} custom-call(s32[1]{0:T(128)} %bitcast.place_ref, s32[2]{0:T(128)S(1)} %pad_add_fusion.device_ref, s32[8]{0:T(128)S(1)} %copy-done.1, f32[2,32,1024]{2,1,0:T(8,128)S(1)} %copy-done, f32[2,32,1024]{2,1,0:T(8,128)S(1)} %get-tuple-element.41.own_ref, bf16[2,32,1024]{2,1,0:T(8,128)(2,1)S(1)} %collective-permute-done.9.refs_0_, ...), custom_call_target="tpu_custom_call" | custom-call | flops 1000000 | bytes 1048576 | tf_op jit(solution)/shard_map/pallas_call | solution.py:266
  (6 shorter events, 0.1 us)
Async XLA Ops:
  0.0 24.9 %copy-start.5 = (f32[8,31]{1,0:T(8,128)S(1)}, f32[8,31]{1,0:T(8,128)}, u32[]{:S(2)}) copy-start(f32[8,31]{1,0:T(8,128)} %kz_ref.1) | copy-start | bytes 2980
  0.0 24.9 %copy-start.4 = (f32[8,31]{1,0:T(8,128)S(1)}, f32[8,31]{1,0:T(8,128)}, u32[]{:S(2)}) copy-start(f32[8,31]{1,0:T(8,128)} %ky_ref.1) | copy-start | bytes 2980
  0.0 24.9 %copy-start.3 = (f32[8,31]{1,0:T(8,128)S(1)}, f32[8,31]{1,0:T(8,128)}, u32[]{:S(2)}) copy-start(f32[8,31]{1,0:T(8,128)} %kx_ref.1) | copy-start | bytes 2980
  0.0 26.5 %copy-start.1 = (s32[8]{0:T(128)S(1)}, s32[8]{0:T(128)}, u32[]{:S(2)}) copy-start(s32[8]{0:T(128)} %offsets_ref.3) | copy-start | bytes 100
  0.0 26.5 %copy-start.2 = (bf16[8,2,32,1024]{3,2,1,0:T(8,128)(2,1)S(1)}, bf16[8,2,32,1024]{3,2,1,0:T(8,128)(2,1)}, u32[]{:S(2)}) copy-start(bf16[8,2,32,1024]{3,2,1,0:T(8,128)(2,1)} %param.7) | copy-start | bytes 3145732
  1.1 11.9 %collective-permute-start.6 = (bf16[2,16,1024]{2,1,0:T(8,128)(2,1)S(1)}, bf16[2,16,1024]{2,1,0:T(8,128)(2,1)S(1)}, u32[]{:S(2)}, u32[]{:S(2)}) collective-permute-start(bf16[2,16,1024]{2,1,0:T(8,128)(2,1)S(1)} %slice_select_fusion.1), channel_id=1, source_target_pairs={{4,11},{5,10},{6,9},{7,8},{8,7},{9,6},{10,5},{11,4},{12,19},{13,18... | collective-permute-start | bytes 196616 | tf_op jit(solution)/shard_map/ppermute | solution.py:224
  5.8 12.3 %collective-permute-start.5 = (bf16[2,16,1024]{2,1,0:T(8,128)(2,1)S(1)}, bf16[2,16,1024]{2,1,0:T(8,128)(2,1)S(1)}, u32[]{:S(2)}, u32[]{:S(2)}) collective-permute-start(bf16[2,16,1024]{2,1,0:T(8,128)(2,1)S(1)} %slice_select_fusion.1), channel_id=1, source_target_pairs={{4,10},{5,11},{6,8},{7,9},{8,6},{9,7},{10,4},{11,5},{12,18},{13,19... | collective-permute-start | bytes 196616 | tf_op jit(solution)/shard_map/ppermute | solution.py:224
  9.3 15.3 %collective-permute-start.2 = (bf16[2,32,1024]{2,1,0:T(8,128)(2,1)S(1)}, bf16[2,32,1024]{2,1,0:T(8,128)(2,1)S(1)}, u32[]{:S(2)}, u32[]{:S(2)}) collective-permute-start(bf16[2,32,1024]{2,1,0:T(8,128)(2,1)S(1)} %convert_element_type.3.refs_0_), channel_id=1, source_target_pairs={{0,3},{1,2},{2,1},{3,0},{4,7},{5,6},{6,5},{7,4},{8,11},{9,10},{10,... | collective-permute-start | bytes 393224 | tf_op jit(solution)/shard_map/ppermute | solution.py:219
  11.8 12.8 %collective-permute-start.1 = (bf16[2,32,1024]{2,1,0:T(8,128)(2,1)S(1)}, bf16[2,32,1024]{2,1,0:T(8,128)(2,1)S(1)}, u32[]{:S(2)}, u32[]{:S(2)}) collective-permute-start(bf16[2,32,1024]{2,1,0:T(8,128)(2,1)S(1)} %convert_element_type.3.refs_0_), channel_id=1, source_target_pairs={{0,2},{1,3},{2,0},{3,1},{4,6},{5,7},{6,4},{7,5},{8,10},{9,11},{10,... | collective-permute-start | bytes 393224 | tf_op jit(solution)/shard_map/ppermute | solution.py:219
  12.1 12.5 %collective-permute-start = (bf16[2,32,1024]{2,1,0:T(8,128)(2,1)S(1)}, bf16[2,32,1024]{2,1,0:T(8,128)(2,1)S(1)}, u32[]{:S(2)}, u32[]{:S(2)}) collective-permute-start(bf16[2,32,1024]{2,1,0:T(8,128)(2,1)S(1)} %convert_element_type.3.refs_0_), channel_id=1, source_target_pairs={{0,1},{1,0},{2,3},{3,2},{4,5},{5,4},{6,7},{7,6},{8,9},{9,8},{10,11... | collective-permute-start | bytes 393224 | tf_op jit(solution)/shard_map/ppermute | solution.py:219
  13.0 10.0 %collective-permute-start.4 = (bf16[2,16,1024]{2,1,0:T(8,128)(2,1)S(1)}, bf16[2,16,1024]{2,1,0:T(8,128)(2,1)S(1)}, u32[]{:S(2)}, u32[]{:S(2)}) collective-permute-start(bf16[2,16,1024]{2,1,0:T(8,128)(2,1)S(1)} %slice_select_fusion.1), channel_id=1, source_target_pairs={{4,9},{5,8},{6,11},{7,10},{8,5},{9,4},{10,7},{11,6},{12,17},{13,16... | collective-permute-start | bytes 196616 | tf_op jit(solution)/shard_map/ppermute | solution.py:224
  18.1 6.5 %collective-permute-start.3 = (bf16[2,16,1024]{2,1,0:T(8,128)(2,1)S(1)}, bf16[2,16,1024]{2,1,0:T(8,128)(2,1)S(1)}, u32[]{:S(2)}, u32[]{:S(2)}) collective-permute-start(bf16[2,16,1024]{2,1,0:T(8,128)(2,1)S(1)} %slice_select_fusion.1), channel_id=1, source_target_pairs={{4,8},{5,9},{6,10},{7,11},{8,4},{9,5},{10,6},{11,7},{12,16},{13,17... | collective-permute-start | bytes 196616 | tf_op jit(solution)/shard_map/ppermute | solution.py:224
  24.7 1.8 %collective-permute-start.7 = (bf16[8,16,1024]{2,1,0:T(8,128)(2,1)S(1)}, bf16[8,16,1024]{2,1,0:T(8,128)(2,1)S(1)}, u32[]{:S(2)}, u32[]{:S(2)}) collective-permute-start(bf16[8,16,1024]{2,1,0:T(8,128)(2,1)S(1)} %slice_select_fusion), channel_id=1, source_target_pairs={{0,4},{4,0},{8,12},{12,8},{16,20},{20,16},{24,28},{28,24},{1,5},{5... | collective-permute-start | bytes 786440 | tf_op jit(solution)/shard_map/ppermute | solution.py:227
  26.6 32.6 %copy-start = (f32[2,32,1024]{2,1,0:T(8,128)S(1)}, f32[2,32,1024]{2,1,0:T(8,128)}, u32[]{:S(2)}) copy-start(f32[2,32,1024]{2,1,0:T(8,128)} %estimate_ref.1) | copy-start | bytes 786436
  30.5 13.0 %collective-permute-start.8 = (bf16[8,16,1024]{2,1,0:T(8,128)(2,1)S(1)}, bf16[8,16,1024]{2,1,0:T(8,128)(2,1)S(1)}, u32[]{:S(2)}, u32[]{:S(2)}) collective-permute-start(bf16[8,16,1024]{2,1,0:T(8,128)(2,1)S(1)} %get-tuple-element.40), channel_id=1, source_target_pairs={{0,4},{4,0},{8,12},{12,8},{16,20},{20,16},{24,28},{28,24},{1,5},{5... | collective-permute-start | bytes 786440 | tf_op jit(solution)/shard_map/ppermute | solution.py:227
  31.0 15.9 %collective-permute-start.12 = (bf16[2,16,1024]{2,1,0:T(8,128)(2,1)S(1)}, bf16[2,16,1024]{2,1,0:T(8,128)(2,1)S(1)}, u32[]{:S(2)}, u32[]{:S(2)}) collective-permute-start(bf16[2,16,1024]{2,1,0:T(8,128)(2,1)S(1)} %get-tuple-element.45), channel_id=1, source_target_pairs={{4,11},{5,10},{6,9},{7,8},{8,7},{9,6},{10,5},{11,4},{12,19},{13,18... | collective-permute-start | bytes 196616 | tf_op jit(solution)/shard_map/ppermute | solution.py:224
  36.0 15.5 %collective-permute-start.13 = (bf16[2,16,1024]{2,1,0:T(8,128)(2,1)S(1)}, bf16[2,16,1024]{2,1,0:T(8,128)(2,1)S(1)}, u32[]{:S(2)}, u32[]{:S(2)}) collective-permute-start(bf16[2,16,1024]{2,1,0:T(8,128)(2,1)S(1)} %get-tuple-element.46), channel_id=1, source_target_pairs={{4,10},{5,11},{6,8},{7,9},{8,6},{9,7},{10,4},{11,5},{12,18},{13,19... | collective-permute-start | bytes 196616 | tf_op jit(solution)/shard_map/ppermute | solution.py:224
  44.2 13.8 %collective-permute-start.9 = (bf16[2,32,1024]{2,1,0:T(8,128)(2,1)S(1)}, bf16[2,32,1024]{2,1,0:T(8,128)(2,1)S(1)}, u32[]{:S(2)}, u32[]{:S(2)}) collective-permute-start(bf16[2,32,1024]{2,1,0:T(8,128)(2,1)S(1)} %get-tuple-element.42), channel_id=1, source_target_pairs={{0,1},{1,0},{2,3},{3,2},{4,5},{5,4},{6,7},{7,6},{8,9},{9,8},{10,11... | collective-permute-start | bytes 393224 | tf_op jit(solution)/shard_map/ppermute | solution.py:219
  44.3 13.7 %collective-permute-start.10 = (bf16[2,32,1024]{2,1,0:T(8,128)(2,1)S(1)}, bf16[2,32,1024]{2,1,0:T(8,128)(2,1)S(1)}, u32[]{:S(2)}, u32[]{:S(2)}) collective-permute-start(bf16[2,32,1024]{2,1,0:T(8,128)(2,1)S(1)} %get-tuple-element.43), channel_id=1, source_target_pairs={{0,2},{1,3},{2,0},{3,1},{4,6},{5,7},{6,4},{7,5},{8,10},{9,11},{10,... | collective-permute-start | bytes 393224 | tf_op jit(solution)/shard_map/ppermute | solution.py:219
  45.4 13.8 %collective-permute-start.11 = (bf16[2,32,1024]{2,1,0:T(8,128)(2,1)S(1)}, bf16[2,32,1024]{2,1,0:T(8,128)(2,1)S(1)}, u32[]{:S(2)}, u32[]{:S(2)}) collective-permute-start(bf16[2,32,1024]{2,1,0:T(8,128)(2,1)S(1)} %get-tuple-element.44), channel_id=1, source_target_pairs={{0,3},{1,2},{2,1},{3,0},{4,7},{5,6},{6,5},{7,4},{8,11},{9,10},{10,... | collective-permute-start | bytes 393224 | tf_op jit(solution)/shard_map/ppermute | solution.py:219
  46.9 9.4 %collective-permute-start.14 = (bf16[2,16,1024]{2,1,0:T(8,128)(2,1)S(1)}, bf16[2,16,1024]{2,1,0:T(8,128)(2,1)S(1)}, u32[]{:S(2)}, u32[]{:S(2)}) collective-permute-start(bf16[2,16,1024]{2,1,0:T(8,128)(2,1)S(1)} %get-tuple-element.47), channel_id=1, source_target_pairs={{4,9},{5,8},{6,11},{7,10},{8,5},{9,4},{10,7},{11,6},{12,17},{13,16... | collective-permute-start | bytes 196616 | tf_op jit(solution)/shard_map/ppermute | solution.py:224
  51.5 6.5 %collective-permute-start.15 = (bf16[2,16,1024]{2,1,0:T(8,128)(2,1)S(1)}, bf16[2,16,1024]{2,1,0:T(8,128)(2,1)S(1)}, u32[]{:S(2)}, u32[]{:S(2)}) collective-permute-start(bf16[2,16,1024]{2,1,0:T(8,128)(2,1)S(1)} %get-tuple-element.48), channel_id=1, source_target_pairs={{4,8},{5,9},{6,10},{7,11},{8,4},{9,5},{10,6},{11,7},{12,16},{13,17... | collective-permute-start | bytes 196616 | tf_op jit(solution)/shard_map/ppermute | solution.py:224

commit v3 on v2

v3 whole, which is shorter than its diff:
```python
import functools
import jax
import jax.numpy as jnp
from jax import lax
from jax.experimental import pallas as pl
from jax.experimental.pallas import tpu as pltpu
from jax.sharding import PartitionSpec as P

F32, BF16 = jnp.float32, jnp.bfloat16
HALO = 16
LANES = 128
WIDE = 256
VMEM_LIMIT = 40 * 1024 * 1024


def normalized(ref):
    return ref[...] / jnp.sum(ref[...], axis=1, keepdims=True)


def select_taps(index, kernel):
    total = jnp.zeros((kernel.shape[0],) + index.shape[1:], F32)
    for tap in range(kernel.shape[1]):
        total = total + jnp.where(index == tap, kernel[:, tap : tap + 1], 0.0)
    return total


def slanted(row, rows):
    spread = jnp.broadcast_to(row, (rows, row.shape[1]))
    return pltpu.roll(spread, 0, 1, stride=1, stride_axis=0)


def matrices_kernel(planes, strip, device_ref, kx_ref, ky_ref, kz_ref, w_ref, wt_ref, tf_ref, tb_ref):
    views, taps = kx_ref.shape
    margin = taps // 2
    extent = strip + 2 * HALO
    kx, ky, kz = normalized(kx_ref), normalized(ky_ref), normalized(kz_ref)
    lane = lax.broadcasted_iota(jnp.int32, (1, LANES), 1)
    x_row = select_taps(lane % extent - (HALO - margin), kx)
    near = jnp.where(lane < LANES // 2, lane, lane - LANES)
    forward_row = select_taps(margin - near, ky)
    backward_row = select_taps(margin + near, ky)
    column = lax.broadcasted_iota(jnp.int32, (1, w_ref.shape[1]), 1) // extent
    device, odd = device_ref[0], device_ref[1] == 1
    plane = (device ^ (column // planes)) * planes + column % planes
    spot = lax.broadcasted_iota(jnp.int32, (strip, LANES), 1) % extent
    z_rows = [select_taps(plane - (device * planes + own) + margin, kz) for own in range(planes)]
    for view in range(views):
        x_block = slanted(x_row[view : view + 1], strip)
        turned = x_block
        for quarter in range(extent // HALO):
            shift = extent - (2 * quarter + 1) * HALO
            moved = pltpu.roll(x_block, (LANES - shift) % LANES, 1)
            here = jnp.logical_and(spot // HALO == quarter, jnp.logical_not(odd))
            turned = jnp.where(here, moved, turned)
        x_block = turned
        x_block = jnp.concatenate([x_block] * (w_ref.shape[1] // LANES), axis=1)
        for own in range(planes):
            first = (view * planes + own) * strip
            block = x_block * z_rows[own][view : view + 1]
            w_ref[first : first + strip, :] = block.astype(BF16)
    wt_ref[...] = w_ref[...].astype(F32).T.astype(BF16)
    i = lax.broadcasted_iota(jnp.int32, (LANES, LANES), 0)
    j = lax.broadcasted_iota(jnp.int32, (LANES, LANES), 1)
    zeros = jnp.zeros((LANES, LANES), BF16)
    for view in range(views):
        for row, out in ((forward_row, tf_ref), (backward_row, tb_ref)):
            circle = slanted(row[view : view + 1], LANES)
            middle = jnp.where(jnp.abs(j - i) < LANES // 2, circle, 0.0).astype(BF16)
            earlier = jnp.where(i - j > LANES // 2, circle, 0.0).astype(BF16)
            later = jnp.where(j - i > LANES // 2, circle, 0.0).astype(BF16)
            grid = ((earlier, zeros), (middle, earlier), (later, middle), (zeros, later))
            for a, blocks in enumerate(grid):
                for b, block in enumerate(blocks):
                    out[view, a * LANES : (a + 1) * LANES, b * LANES : (b + 1) * LANES] = block


def write_coded(out_ref, where, values):
    pick = values.shape[-1] // 2 - LANES
    base = values[..., pick : pick + LANES].astype(BF16)
    wide = base.astype(F32)
    for first in range(0, values.shape[-1], LANES):
        part = values[..., first : first + LANES]
        part = base if first == pick else (part - wide).astype(BF16)
        out_ref[where + (slice(first, first + LANES),)] = part


def decoded(values, first):
    pick = values.shape[-1] // 2 - LANES
    base = values[..., pick : pick + LANES].astype(F32)
    if first == pick:
        return base
    return base + values[..., first : first + LANES].astype(F32)


def main_kernel(planes, view_rows, place_ref, offsets_ref, *refs):
    quarters, (views_ref, w_ref, wt_ref, tf_ref, tb_ref) = refs[:4], refs[4:9]
    cores, backs, (ext_ref, pad_ref, back_ref, deep_ref) = refs[9:11], refs[11:13], refs[13:]
    views = offsets_ref.shape[0]
    count = quarters[0].shape[0]
    extent = ext_ref.shape[0] // count
    strip = extent - 2 * HALO
    columns = ext_ref.shape[-1]
    group = planes * strip
    for p in range(count):
        for n, ref in enumerate(quarters[::-1]):
            ext_ref[p * extent + n * HALO : p * extent + (n + 1) * HALO, :] = ref[p]
    for pad in (pad_ref, back_ref):
        pad[:, :LANES] = jnp.zeros((pad.shape[0], LANES), BF16)
        pad[:, LANES + columns :] = jnp.zeros((pad.shape[0], LANES), BF16)
    for first in range(0, columns, WIDE):
        block = jnp.dot(w_ref[...], ext_ref[:, first : first + WIDE], preferred_element_type=F32)
        pad_ref[:, LANES + first : LANES + first + WIDE] = block.astype(BF16)
    row = place_ref[0] + lax.broadcasted_iota(jnp.int32, (group, WIDE), 0) % strip
    starts = range(0, columns, WIDE)

    def windows(pad, rows):
        return jnp.concatenate([pad[rows, first : first + WIDE + 2 * LANES] for first in starts], axis=0)

    for view in range(views):
        rows = slice(view * group, (view + 1) * group)
        low = offsets_ref[view]
        inside = (row >= low) & (row < low + view_rows)
        blurred = jnp.dot(windows(pad_ref, rows), tf_ref[view], preferred_element_type=F32)
        for n, first in enumerate(starts):
            part = blurred[n * group : (n + 1) * group]
            seen = views_ref[rows, first : first + WIDE].astype(F32)
            correction = jnp.where(inside, seen / part - 1.0, 0.0)
            back_ref[rows, LANES + first : LANES + first + WIDE] = correction.astype(BF16)
        backward = jnp.dot(windows(back_ref, rows), tb_ref[view], preferred_element_type=F32)
        for n, first in enumerate(starts):
            deep_ref[rows, first : first + WIDE] = backward[n * group : (n + 1) * group].astype(BF16)
    for p in range(count):
        part = jnp.dot(wt_ref[p * extent : (p + 1) * extent], deep_ref[...], preferred_element_type=F32)
        write_coded(backs[0], (p, slice(None)), part[:HALO])
        cores[0][p] = part[HALO : 2 * HALO]
        cores[1][p] = part[2 * HALO : 3 * HALO]
        write_coded(backs[1], (p, slice(None)), part[3 * HALO :])


def join_kernel(planes, core_ref, other_ref, own_ref, *sends):
    columns = core_ref.shape[2]
    for p in range(core_ref.shape[0]):
        other = other_ref[p]
        parts = []
        for first in range(0, columns, LANES):
            parts.append(core_ref[p, :, first : first + LANES] + decoded(other, first))
        whole = jnp.concatenate(parts, axis=1)
        if p < planes:
            own_ref[p] = whole
        else:
            write_coded(sends[p // planes - 1], (p % planes, slice(None)), whole)


def update_kernel(view_rows, place_ref, device_ref, offsets_ref, estimate_ref, *refs):
    parts, out_ref = refs[:-1], refs[-1]
    planes, strip, columns = estimate_ref.shape
    odd = device_ref[1]
    for half, start in ((0, (1 - odd) * HALO), (1, odd * HALO)):
        mine = parts[half * (len(parts) // 2) : (half + 1) * (len(parts) // 2)]
        row = place_ref[0] + start + lax.broadcasted_iota(jnp.int32, (HALO, LANES), 0)
        coverage = jnp.zeros((HALO, LANES), F32)
        for view in range(offsets_ref.shape[0]):
            low = offsets_ref[view]
            coverage = coverage + jnp.where((row >= low) & (row < low + view_rows), 1.0, 0.0)
        scale = 1.0 / jnp.maximum(coverage, 1.0)
        rows = pl.ds(pl.multiple_of(start, HALO), HALO)
        for p in range(planes):
            for first in range(0, columns, LANES):
                lanes = slice(first, first + LANES)
                summed = mine[0][p, :, lanes]
                for ref in mine[1:]:
                    summed = summed + decoded(ref[p], first)
                out_ref[p, rows, lanes] = estimate_ref[p, rows, lanes] * (1.0 + summed * scale)


def call(body, outs, scalars, arrays, scratch=(), flops=0, moved=0):
    return pl.pallas_call(
        body,
        out_shape=outs,
        in_specs=[pl.BlockSpec(memory_space=pltpu.SMEM)] * scalars
        + [pl.BlockSpec(memory_space=pltpu.VMEM)] * arrays,
        out_specs=jax.tree.map(lambda _: pl.BlockSpec(memory_space=pltpu.VMEM), outs),
        scratch_shapes=list(scratch),
        compiler_params=pltpu.CompilerParams(vmem_limit_bytes=VMEM_LIMIT),
        cost_estimate=pl.CostEstimate(flops=flops, bytes_accessed=moved, transcendentals=0),
    )


def shards(estimate, views, kernel_x, kernel_y, kernel_z, offsets):
    shape = jax.ShapeDtypeStruct
    depth, tiles = lax.axis_size("depth"), lax.axis_size("tile")
    planes, strip, columns = estimate.shape
    count = views.shape[0]
    extent = strip + 2 * HALO
    rows = count * planes * strip
    span = depth * planes * extent
    view_rows = 5 * strip * tiles // 8
    tile = lax.axis_index("tile").astype(jnp.int32)
    odd = tile % 2
    place = (tile * strip).reshape(1)
    device = jnp.stack([lax.axis_index("depth").astype(jnp.int32), odd])
    assert strip == 2 * HALO and tiles % 2 == 0

    def across(array, step):
        return lax.ppermute(array, "depth", [(i, i ^ step) for i in range(depth)])

    def beside(array):
        return lax.ppermute(array, "tile", [(i, i - 1 + 2 * (i % 2)) for i in range(1, tiles - 1)])

    def within(array):
        return lax.ppermute(array, "tile", [(i, i ^ 1) for i in range(tiles)])

    own = estimate.astype(BF16)
    early, late = own[:, :HALO], own[:, HALO:]
    outer_own, inner_own = jnp.where(odd == 1, late, early), jnp.where(odd == 1, early, late)
    outer = jnp.concatenate([outer_own] + [across(outer_own, step) for step in range(1, depth)], axis=0)
    other_chip = beside(outer)
    inner = jnp.concatenate([inner_own] + [across(inner_own, step) for step in range(1, depth)], axis=0)
    other_core = within(inner)
    w, wt, tf, tb = call(
        functools.partial(matrices_kernel, planes, strip),
        (shape((rows, span), BF16), shape((span, rows), BF16))
        + (shape((count, WIDE + 2 * LANES, WIDE), BF16),) * 2,
        1, 3, flops=10**8, moved=5 * 2**20,
    )(device, kernel_x, kernel_y, kernel_z)
    halves = (depth * planes, HALO, columns)
    inner, outer, to_core, to_chip = call(
        functools.partial(main_kernel, planes, view_rows),
        (shape(halves, F32),) * 2 + (shape(halves, BF16),) * 2,
        2, 9,
        scratch=(
            pltpu.VMEM((span, columns), BF16),
            pltpu.VMEM((rows, columns + 2 * LANES), BF16),
            pltpu.VMEM((rows, columns + 2 * LANES), BF16),
            pltpu.VMEM((rows, columns), BF16),
        ),
        flops=2 * 10**9, moved=10 * 2**20,
    )(place, offsets, other_chip, outer, inner, other_core, views.reshape(rows, columns), w, wt, tf, tb)
    block = (planes, HALO, columns)
    sums = []
    for core, other in ((inner, within(to_core)), (outer, beside(to_chip))):
        own_sum, *sends = call(
            functools.partial(join_kernel, planes),
            (shape(block, F32),) + (shape(block, BF16),) * (depth - 1),
            0, 2, flops=10**6, moved=3 * 2**20,
        )(core, other)
        sums += [own_sum] + [across(send, step + 1) for step, send in enumerate(sends)]
    return call(
        functools.partial(update_kernel, view_rows),
        shape(estimate.shape, F32),
        3, 1 + 2 * depth, flops=10**6, moved=2**20,
    )(place, device, offsets, estimate, *sums)


def solution(mesh):
    in_specs = (P("depth", "tile", None), P(None, "depth", "tile", None), P(), P(), P(), P())
    out_specs = P("depth", "tile", None)
    return jax.shard_map(shards, mesh=mesh, in_specs=in_specs, out_specs=out_specs, check_vma=False)
```

time: 60.9 us -> 48.5 us (0.80)
  the two profiles are of different devices: /device:TPU:11 before, /device:TPU:4 now
where the time goes in v3:
time: 48.5 us; the launch traced here: 48.2 us
  starting transfers between devices  22.3 us (46%)
  waiting for transfers between devices  15.1 us (31%)
  Pallas kernels  7.35 us (15%)
  local copies, waits for them, and re-layouts  2.07 us (4%)
  other arithmetic  1.21 us (2%)
    ppermute x12, starting transfers between devices, across(): return lax.ppermute(array, 'depth', [(i, i ^ step) for i in range(depth)])  17.7 us
    ppermute x12, waiting for transfers between devices, across(): return lax.ppermute(array, 'depth', [(i, i ^ step) for i in range(depth)])  9.22 us
    ppermute x2, waiting for transfers between devices, beside(): lax.ppermute(array, 'tile', [(i, i - 1 + 2 * (i % 2)) for i in range(1, t...  5.92 us
    pallas_call x1, Pallas kernels, shards(): call(functools.partial(main_kernel, planes, view_rows), (shape(halves, F3...  3.92 us
    ppermute x2, starting transfers between devices, beside(): lax.ppermute(array, 'tile', [(i, i - 1 + 2 * (i % 2)) for i in range(1, t...  3.86 us
    unnamed x12, local copies, waits for them, and re-layouts  2.07 us
    pallas_call x1, Pallas kernels, shards(): call(functools.partial(matrices_kernel, planes, strip), (shape((rows, spa...  1.88 us
    pallas_call x1, Pallas kernels, shards(): call(functools.partial(update_kernel, view_rows), shape(estimate.shape, F...  1.38 us
  transfers between devices with their start and end apart: 16, of which 7 were waited for; matrix products, arithmetic and copies ran while one was open for 0% of the time, Pallas kernels for 4%

profile of v3, /device:TPU:4, one launch (start us, length us, event | category | flops | bytes accessed | tf_op | source)
XLA Modules:
  0.0 48.2 jit_solution(8269076793421280847)
XLA Ops:
  0.0 0.0 copy-start.1
  0.0 0.0 copy-start.2
  0.0 1.1 %convert_element_type.3 = bf16[2,32,1024]{2,1,0:T(8,128)(2,1)S(1)} convert(f32[2,32,1024]{2,1,0:T(8,128)} %estimate_ref.1) | non-fusion elementwise | flops 65536 | bytes 393216 | tf_op jit(solution)/shard_map/convert_element_type | solution.py:213
  1.1 3.7 %collective-permute-start.2 = (bf16[2,16,1024]{2,1,0:T(8,128)(2,1)S(1)}, bf16[2,16,1024]{2,1,0:T(8,128)(2,1)S(1)}, u32[]{:S(2)}, u32[]{:S(2)}) collective-permute-start(bf16[2,16,1024]{2,1,0:T(8,128)(2,1)S(1)} %get-tuple-element.38), channel_id=1, source_target_pairs={{0,3},{1,2},{2,1},{3,0},{4,7},{5,6},{6,5},{7,4},{8,11},{9,10},{10,... | collective-permute-start | bytes 196616 | tf_op jit(solution)/shard_map/ppermute | solution.py:205
  4.8 0.0 collective-permute-start.1
  4.8 0.8 %collective-permute-start = (bf16[2,16,1024]{2,1,0:T(8,128)(2,1)S(1)}, bf16[2,16,1024]{2,1,0:T(8,128)(2,1)S(1)}, u32[]{:S(2)}, u32[]{:S(2)}) collective-permute-start(bf16[2,16,1024]{2,1,0:T(8,128)(2,1)S(1)} %get-tuple-element.38), channel_id=1, source_target_pairs={{0,1},{1,0},{2,3},{3,2},{4,5},{5,4},{6,7},{7,6},{8,9},{9,8},{10,11... | collective-permute-start | bytes 196616 | tf_op jit(solution)/shard_map/ppermute | solution.py:205
  5.5 3.6 %collective-permute-start.6 = (bf16[2,16,1024]{2,1,0:T(8,128)(2,1)S(1)}, bf16[2,16,1024]{2,1,0:T(8,128)(2,1)S(1)}, u32[]{:S(2)}, u32[]{:S(2)}) collective-permute-start(bf16[2,16,1024]{2,1,0:T(8,128)(2,1)S(1)} %get-tuple-element.37), channel_id=1, source_target_pairs={{0,3},{1,2},{2,1},{3,0},{4,7},{5,6},{6,5},{7,4},{8,11},{9,10},{10,... | collective-permute-start | bytes 196616 | tf_op jit(solution)/shard_map/ppermute | solution.py:205
  9.1 0.0 collective-permute-start.5
  9.1 0.0 collective-permute-done.2
  9.1 0.8 %collective-permute-start.4 = (bf16[2,16,1024]{2,1,0:T(8,128)(2,1)S(1)}, bf16[2,16,1024]{2,1,0:T(8,128)(2,1)S(1)}, u32[]{:S(2)}, u32[]{:S(2)}) collective-permute-start(bf16[2,16,1024]{2,1,0:T(8,128)(2,1)S(1)} %get-tuple-element.37), channel_id=1, source_target_pairs={{0,1},{1,0},{2,3},{3,2},{4,5},{5,4},{6,7},{7,6},{8,9},{9,8},{10,11... | collective-permute-start | bytes 196616 | tf_op jit(solution)/shard_map/ppermute | solution.py:205
  9.9 3.0 %collective-permute-done.1 = bf16[2,16,1024]{2,1,0:T(8,128)(2,1)S(1)} collective-permute-done((bf16[2,16,1024]{2,1,0:T(8,128)(2,1)S(1)}, bf16[2,16,1024]{2,1,0:T(8,128)(2,1)S(1)}, u32[]{:S(2)}, u32[]{:S(2)}) %collective-permute-start.1) | collective-permute-done | bytes 65568 | tf_op jit(solution)/shard_map/ppermute | solution.py:205
  13.0 0.0 collective-permute-done
  13.0 1.9 %collective-permute-start.3 = (bf16[8,16,1024]{2,1,0:T(8,128)(2,1)S(1)}, bf16[8,16,1024]{2,1,0:T(8,128)(2,1)S(1)}, u32[]{:S(2)}, u32[]{:S(2)}) collective-permute-start(bf16[8,16,1024]{2,1,0:T(8,128)(2,1)S(1)} %pad_maximum_fusion.refs_1_), channel_id=1, source_target_pairs={{4,8},{8,4},{12,16},{16,12},{20,24},{24,20},{5,9},{9,5},{13,17},{1... | collective-permute-start | bytes 786440 | tf_op jit(solution)/shard_map/ppermute | solution.py:208
  14.9 0.0 collective-permute-done.6
  15.0 1.0 %collective-permute-done.5 = bf16[2,16,1024]{2,1,0:T(8,128)(2,1)S(1)} collective-permute-done((bf16[2,16,1024]{2,1,0:T(8,128)(2,1)S(1)}, bf16[2,16,1024]{2,1,0:T(8,128)(2,1)S(1)}, u32[]{:S(2)}, u32[]{:S(2)}) %collective-permute-start.5) | collective-permute-done | bytes 65568 | tf_op jit(solution)/shard_map/ppermute | solution.py:205
  16.0 0.0 collective-permute-done.4
  16.0 0.7 %collective-permute-start.7 = (bf16[8,16,1024]{2,1,0:T(8,128)(2,1)S(1)}, bf16[8,16,1024]{2,1,0:T(8,128)(2,1)S(1)}, u32[]{:S(2)}, u32[]{:S(2)}) collective-permute-start(bf16[8,16,1024]{2,1,0:T(8,128)(2,1)S(1)} %pad_maximum_fusion.1.refs_2_), channel_id=1, source_target_pairs={{0,4},{4,0},{8,12},{12,8},{16,20},{20,16},{24,28},{28,24},{1,5},{5... | collective-permute-start | bytes 786440 | tf_op jit(solution)/shard_map/ppermute | solution.py:211
  16.7 0.1 pad_add_fusion.device_ref
  16.8 0.0 copy-start.3
  16.8 0.7 %copy-done.3 = f32[8,31]{1,0:T(8,128)S(1)} copy-done((f32[8,31]{1,0:T(8,128)S(1)}, f32[8,31]{1,0:T(8,128)}, u32[]{:S(2)}) %copy-start.3) | copy-done | bytes 1016
  17.4 0.0 copy-start.4
  17.4 0.7 %copy-done.4 = f32[8,31]{1,0:T(8,128)S(1)} copy-done((f32[8,31]{1,0:T(8,128)S(1)}, f32[8,31]{1,0:T(8,128)}, u32[]{:S(2)}) %copy-start.4) | copy-done | bytes 1016
  18.1 0.0 copy-start.5
  18.1 0.7 %copy-done.5 = f32[8,31]{1,0:T(8,128)S(1)} copy-done((f32[8,31]{1,0:T(8,128)S(1)}, f32[8,31]{1,0:T(8,128)}, u32[]{:S(2)}) %copy-start.5) | copy-done | bytes 1016
  18.8 1.9 %shard_map.64 = (bf16[512,512]{1,0:T(8,128)(2,1)S(1)}, bf16[512,512]{1,0:T(8,128)(2,1)S(1)}, bf16[8,512,256]{2,1,0:T(8,128)(2,1)S(1)}, bf16[8,512,256]{2,1,0:T(8,128)(2,1)S(1)}) custom-call(s32[2]{0:T(128)S(1)} %pad_add_fusion.device_ref, f32[8,31]{1,0:T(8,128)S(1)} %copy-done.3, f32[8,31]{1,0:T(8,128)S(1)} %copy-done.4, f32[8,31]{1,0:T(8,128)S(1)} %copy-done.5), custom_call_target="tpu_custom_call" | custom-call | flops 100000000 | bytes 5242880 | tf_op jit(solution)/shard_map/pallas_call | solution.py:220
  20.7 2.8 %collective-permute-done.3.refs_0_ = bf16[8,16,1024]{2,1,0:T(8,128)(2,1)S(1)} collective-permute-done((bf16[8,16,1024]{2,1,0:T(8,128)(2,1)S(1)}, bf16[8,16,1024]{2,1,0:T(8,128)(2,1)S(1)}, u32[]{:S(2)}, u32[]{:S(2)}) %collective-permute-start.3) | collective-permute-done | bytes 262176 | tf_op jit(solution)/shard_map/ppermute | solution.py:208
  23.5 0.0 collective-permute-done.7.refs_3_
  23.5 0.0 copy-done.1
  23.5 0.0 copy-done.2
  23.5 0.0 copy-start
  23.5 3.9 %shard_map.65 = (f32[8,16,1024]{2,1,0:T(8,128)S(1)}, f32[8,16,1024]{2,1,0:T(8,128)S(1)}, bf16[8,16,1024]{2,1,0:T(8,128)(2,1)S(1)}, bf16[8,16,1024]{2,1,0:T(8,128)(2,1)S(1)}) custom-call(s32[1]{0:T(128)} %bitcast.place_ref, s32[8]{0:T(128)S(1)} %copy-done.1, bf16[8,16,1024]{2,1,0:T(8,128)(2,1)S(1)} %collective-permute-done.3.refs_0_, ...), custom_call_target="tpu_custom_call" | custom-call | flops 2000000000 | bytes 10485760 | tf_op jit(solution)/shard_map/pallas_call | solution.py:227
  27.5 0.1 collective-permute-start.8
  27.5 1.9 %collective-permute-start.12 = (bf16[8,16,1024]{2,1,0:T(8,128)(2,1)S(1)}, bf16[8,16,1024]{2,1,0:T(8,128)(2,1)S(1)}, u32[]{:S(2)}, u32[]{:S(2)}) collective-permute-start(bf16[8,16,1024]{2,1,0:T(8,128)(2,1)S(1)} %get-tuple-element.32), channel_id=1, source_target_pairs={{4,8},{8,4},{12,16},{16,12},{20,24},{24,20},{5,9},{9,5},{13,17},{1... | collective-permute-start | bytes 786440 | tf_op jit(solution)/shard_map/ppermute | solution.py:208
  29.5 0.0 collective-permute-done.8.other_ref
  29.5 0.1 shard_map.66
  29.6 0.1 collective-permute-start.9
  29.7 3.5 %collective-permute-start.10 = (bf16[2,16,1024]{2,1,0:T(8,128)(2,1)S(1)}, bf16[2,16,1024]{2,1,0:T(8,128)(2,1)S(1)}, u32[]{:S(2)}, u32[]{:S(2)}) collective-permute-start(bf16[2,16,1024]{2,1,0:T(8,128)(2,1)S(1)} %get-tuple-element.29), channel_id=1, source_target_pairs={{0,2},{1,3},{2,0},{3,1},{4,6},{5,7},{6,4},{7,5},{8,10},{9,11},{10,... | collective-permute-start | bytes 196616 | tf_op jit(solution)/shard_map/ppermute | solution.py:205
  33.1 0.9 %collective-permute-start.11 = (bf16[2,16,1024]{2,1,0:T(8,128)(2,1)S(1)}, bf16[2,16,1024]{2,1,0:T(8,128)(2,1)S(1)}, u32[]{:S(2)}, u32[]{:S(2)}) collective-permute-start(bf16[2,16,1024]{2,1,0:T(8,128)(2,1)S(1)} %get-tuple-element.30), channel_id=1, source_target_pairs={{0,3},{1,2},{2,1},{3,0},{4,7},{5,6},{6,5},{7,4},{8,11},{9,10},{10,... | collective-permute-start | bytes 196616 | tf_op jit(solution)/shard_map/ppermute | solution.py:205
  34.0 3.1 %collective-permute-done.12.other_ref = bf16[8,16,1024]{2,1,0:T(8,128)(2,1)S(1)} collective-permute-done((bf16[8,16,1024]{2,1,0:T(8,128)(2,1)S(1)}, bf16[8,16,1024]{2,1,0:T(8,128)(2,1)S(1)}, u32[]{:S(2)}, u32[]{:S(2)}) %collective-permute-start.12) | collective-permute-done | bytes 262176 | tf_op jit(solution)/shard_map/ppermute | solution.py:208
  37.2 0.1 shard_map.67
  37.2 0.1 collective-permute-start.13
  37.3 3.5 %collective-permute-start.14 = (bf16[2,16,1024]{2,1,0:T(8,128)(2,1)S(1)}, bf16[2,16,1024]{2,1,0:T(8,128)(2,1)S(1)}, u32[]{:S(2)}, u32[]{:S(2)}) collective-permute-start(bf16[2,16,1024]{2,1,0:T(8,128)(2,1)S(1)} %get-tuple-element.35), channel_id=1, source_target_pairs={{0,2},{1,3},{2,0},{3,1},{4,6},{5,7},{6,4},{7,5},{8,10},{9,11},{10,... | collective-permute-start | bytes 196616 | tf_op jit(solution)/shard_map/ppermute | solution.py:205
  40.8 0.0 collective-permute-done.9.refs_1_
  40.8 0.9 %collective-permute-start.15 = (bf16[2,16,1024]{2,1,0:T(8,128)(2,1)S(1)}, bf16[2,16,1024]{2,1,0:T(8,128)(2,1)S(1)}, u32[]{:S(2)}, u32[]{:S(2)}) collective-permute-start(bf16[2,16,1024]{2,1,0:T(8,128)(2,1)S(1)} %get-tuple-element.36), channel_id=1, source_target_pairs={{0,3},{1,2},{2,1},{3,0},{4,7},{5,6},{6,5},{7,4},{8,11},{9,10},{10,... | collective-permute-start | bytes 196616 | tf_op jit(solution)/shard_map/ppermute | solution.py:205
  41.7 0.0 collective-permute-done.10.refs_2_
  41.7 0.0 collective-permute-done.11.refs_3_
  41.7 0.2 collective-permute-done.13.refs_5_
  41.9 1.4 %collective-permute-done.14.refs_6_ = bf16[2,16,1024]{2,1,0:T(8,128)(2,1)S(1)} collective-permute-done((bf16[2,16,1024]{2,1,0:T(8,128)(2,1)S(1)}, bf16[2,16,1024]{2,1,0:T(8,128)(2,1)S(1)}, u32[]{:S(2)}, u32[]{:S(2)}) %collective-permute-start.14) | collective-permute-done | bytes 65568 | tf_op jit(solution)/shard_map/ppermute | solution.py:205
  43.3 3.6 %collective-permute-done.15.refs_7_ = bf16[2,16,1024]{2,1,0:T(8,128)(2,1)S(1)} collective-permute-done((bf16[2,16,1024]{2,1,0:T(8,128)(2,1)S(1)}, bf16[2,16,1024]{2,1,0:T(8,128)(2,1)S(1)}, u32[]{:S(2)}, u32[]{:S(2)}) %collective-permute-start.15) | collective-permute-done | bytes 65568 | tf_op jit(solution)/shard_map/ppermute | solution.py:205
  46.8 0.0 copy-done
  46.9 1.4 %shard_map.68 = f32[2,32,1024]{2,1,0:T(8,128)} custom-call(s32[1]{0:T(128)} %bitcast.place_ref, s32[2]{0:T(128)S(1)} %pad_add_fusion.device_ref, s32[8]{0:T(128)S(1)} %copy-done.1, f32[2,32,1024]{2,1,0:T(8,128)S(1)} %copy-done, f32[2,16,1024]{2,1,0:T(8,128)S(1)} %get-tuple-element.27.refs_0_, bf16[2,16,1024]{2,1,0:T(8,128)(2,1)S(1)} %collective-permute-done.9.refs_1_, ...), custom_call_target="tpu_custom_call" | custom-call | flops 1000000 | bytes 1048576 | tf_op jit(solution)/shard_map/pallas_call | solution.py:248
  (3 shorter events, 0.1 us)
Async XLA Ops:
  0.0 23.5 %copy-start.1 = (s32[8]{0:T(128)S(1)}, s32[8]{0:T(128)}, u32[]{:S(2)}) copy-start(s32[8]{0:T(128)} %offsets_ref.3) | copy-start | bytes 100
  0.0 23.5 %copy-start.2 = (bf16[8,2,32,1024]{3,2,1,0:T(8,128)(2,1)S(1)}, bf16[8,2,32,1024]{3,2,1,0:T(8,128)(2,1)}, u32[]{:S(2)}) copy-start(bf16[8,2,32,1024]{3,2,1,0:T(8,128)(2,1)} %param.7) | copy-start | bytes 3145732
  1.1 8.1 %collective-permute-start.2 = (bf16[2,16,1024]{2,1,0:T(8,128)(2,1)S(1)}, bf16[2,16,1024]{2,1,0:T(8,128)(2,1)S(1)}, u32[]{:S(2)}, u32[]{:S(2)}) collective-permute-start(bf16[2,16,1024]{2,1,0:T(8,128)(2,1)S(1)} %get-tuple-element.38), channel_id=1, source_target_pairs={{0,3},{1,2},{2,1},{3,0},{4,7},{5,6},{6,5},{7,4},{8,11},{9,10},{10,... | collective-permute-start | bytes 196616 | tf_op jit(solution)/shard_map/ppermute | solution.py:205
  4.8 8.2 %collective-permute-start.1 = (bf16[2,16,1024]{2,1,0:T(8,128)(2,1)S(1)}, bf16[2,16,1024]{2,1,0:T(8,128)(2,1)S(1)}, u32[]{:S(2)}, u32[]{:S(2)}) collective-permute-start(bf16[2,16,1024]{2,1,0:T(8,128)(2,1)S(1)} %get-tuple-element.38), channel_id=1, source_target_pairs={{0,2},{1,3},{2,0},{3,1},{4,6},{5,7},{6,4},{7,5},{8,10},{9,11},{10,... | collective-permute-start | bytes 196616 | tf_op jit(solution)/shard_map/ppermute | solution.py:205
  4.8 8.2 %collective-permute-start = (bf16[2,16,1024]{2,1,0:T(8,128)(2,1)S(1)}, bf16[2,16,1024]{2,1,0:T(8,128)(2,1)S(1)}, u32[]{:S(2)}, u32[]{:S(2)}) collective-permute-start(bf16[2,16,1024]{2,1,0:T(8,128)(2,1)S(1)} %get-tuple-element.38), channel_id=1, source_target_pairs={{0,1},{1,0},{2,3},{3,2},{4,5},{5,4},{6,7},{7,6},{8,9},{9,8},{10,11... | collective-permute-start | bytes 196616 | tf_op jit(solution)/shard_map/ppermute | solution.py:205
  5.5 9.4 %collective-permute-start.6 = (bf16[2,16,1024]{2,1,0:T(8,128)(2,1)S(1)}, bf16[2,16,1024]{2,1,0:T(8,128)(2,1)S(1)}, u32[]{:S(2)}, u32[]{:S(2)}) collective-permute-start(bf16[2,16,1024]{2,1,0:T(8,128)(2,1)S(1)} %get-tuple-element.37), channel_id=1, source_target_pairs={{0,3},{1,2},{2,1},{3,0},{4,7},{5,6},{6,5},{7,4},{8,11},{9,10},{10,... | collective-permute-start | bytes 196616 | tf_op jit(solution)/shard_map/ppermute | solution.py:205
  9.1 6.8 %collective-permute-start.5 = (bf16[2,16,1024]{2,1,0:T(8,128)(2,1)S(1)}, bf16[2,16,1024]{2,1,0:T(8,128)(2,1)S(1)}, u32[]{:S(2)}, u32[]{:S(2)}) collective-permute-start(bf16[2,16,1024]{2,1,0:T(8,128)(2,1)S(1)} %get-tuple-element.37), channel_id=1, source_target_pairs={{0,2},{1,3},{2,0},{3,1},{4,6},{5,7},{6,4},{7,5},{8,10},{9,11},{10,... | collective-permute-start | bytes 196616 | tf_op jit(solution)/shard_map/ppermute | solution.py:205
  9.1 6.8 %collective-permute-start.4 = (bf16[2,16,1024]{2,1,0:T(8,128)(2,1)S(1)}, bf16[2,16,1024]{2,1,0:T(8,128)(2,1)S(1)}, u32[]{:S(2)}, u32[]{:S(2)}) collective-permute-start(bf16[2,16,1024]{2,1,0:T(8,128)(2,1)S(1)} %get-tuple-element.37), channel_id=1, source_target_pairs={{0,1},{1,0},{2,3},{3,2},{4,5},{5,4},{6,7},{7,6},{8,9},{9,8},{10,11... | collective-permute-start | bytes 196616 | tf_op jit(solution)/shard_map/ppermute | solution.py:205
  13.0 10.5 %collective-permute-start.3 = (bf16[8,16,1024]{2,1,0:T(8,128)(2,1)S(1)}, bf16[8,16,1024]{2,1,0:T(8,128)(2,1)S(1)}, u32[]{:S(2)}, u32[]{:S(2)}) collective-permute-start(bf16[8,16,1024]{2,1,0:T(8,128)(2,1)S(1)} %pad_maximum_fusion.refs_1_), channel_id=1, source_target_pairs={{4,8},{8,4},{12,16},{16,12},{20,24},{24,20},{5,9},{9,5},{13,17},{1... | collective-permute-start | bytes 786440 | tf_op jit(solution)/shard_map/ppermute | solution.py:208
  16.0 7.5 %collective-permute-start.7 = (bf16[8,16,1024]{2,1,0:T(8,128)(2,1)S(1)}, bf16[8,16,1024]{2,1,0:T(8,128)(2,1)S(1)}, u32[]{:S(2)}, u32[]{:S(2)}) collective-permute-start(bf16[8,16,1024]{2,1,0:T(8,128)(2,1)S(1)} %pad_maximum_fusion.1.refs_2_), channel_id=1, source_target_pairs={{0,4},{4,0},{8,12},{12,8},{16,20},{20,16},{24,28},{28,24},{1,5},{5... | collective-permute-start | bytes 786440 | tf_op jit(solution)/shard_map/ppermute | solution.py:211
  16.8 0.7 %copy-start.3 = (f32[8,31]{1,0:T(8,128)S(1)}, f32[8,31]{1,0:T(8,128)}, u32[]{:S(2)}) copy-start(f32[8,31]{1,0:T(8,128)} %kx_ref.1) | copy-start | bytes 2980
  17.4 0.7 %copy-start.4 = (f32[8,31]{1,0:T(8,128)S(1)}, f32[8,31]{1,0:T(8,128)}, u32[]{:S(2)}) copy-start(f32[8,31]{1,0:T(8,128)} %ky_ref.1) | copy-start | bytes 2980
  18.1 0.7 %copy-start.5 = (f32[8,31]{1,0:T(8,128)S(1)}, f32[8,31]{1,0:T(8,128)}, u32[]{:S(2)}) copy-start(f32[8,31]{1,0:T(8,128)} %kz_ref.1) | copy-start | bytes 2980
  23.5 23.3 %copy-start = (f32[2,32,1024]{2,1,0:T(8,128)S(1)}, f32[2,32,1024]{2,1,0:T(8,128)}, u32[]{:S(2)}) copy-start(f32[2,32,1024]{2,1,0:T(8,128)} %estimate_ref.1) | copy-start | bytes 786436
  27.5 2.0 %collective-permute-start.8 = (bf16[8,16,1024]{2,1,0:T(8,128)(2,1)S(1)}, bf16[8,16,1024]{2,1,0:T(8,128)(2,1)S(1)}, u32[]{:S(2)}, u32[]{:S(2)}) collective-permute-start(bf16[8,16,1024]{2,1,0:T(8,128)(2,1)S(1)} %get-tuple-element.26), channel_id=1, source_target_pairs={{0,4},{4,0},{8,12},{12,8},{16,20},{20,16},{24,28},{28,24},{1,5},{5... | collective-permute-start | bytes 786440 | tf_op jit(solution)/shard_map/ppermute | solution.py:211
  27.5 9.6 %collective-permute-start.12 = (bf16[8,16,1024]{2,1,0:T(8,128)(2,1)S(1)}, bf16[8,16,1024]{2,1,0:T(8,128)(2,1)S(1)}, u32[]{:S(2)}, u32[]{:S(2)}) collective-permute-start(bf16[8,16,1024]{2,1,0:T(8,128)(2,1)S(1)} %get-tuple-element.32), channel_id=1, source_target_pairs={{4,8},{8,4},{12,16},{16,12},{20,24},{24,20},{5,9},{9,5},{13,17},{1... | collective-permute-start | bytes 786440 | tf_op jit(solution)/shard_map/ppermute | solution.py:208
  29.6 11.2 %collective-permute-start.9 = (bf16[2,16,1024]{2,1,0:T(8,128)(2,1)S(1)}, bf16[2,16,1024]{2,1,0:T(8,128)(2,1)S(1)}, u32[]{:S(2)}, u32[]{:S(2)}) collective-permute-start(bf16[2,16,1024]{2,1,0:T(8,128)(2,1)S(1)} %get-tuple-element.28), channel_id=1, source_target_pairs={{0,1},{1,0},{2,3},{3,2},{4,5},{5,4},{6,7},{7,6},{8,9},{9,8},{10,11... | collective-permute-start | bytes 196616 | tf_op jit(solution)/shard_map/ppermute | solution.py:205
  29.7 12.0 %collective-permute-start.10 = (bf16[2,16,1024]{2,1,0:T(8,128)(2,1)S(1)}, bf16[2,16,1024]{2,1,0:T(8,128)(2,1)S(1)}, u32[]{:S(2)}, u32[]{:S(2)}) collective-permute-start(bf16[2,16,1024]{2,1,0:T(8,128)(2,1)S(1)} %get-tuple-element.29), channel_id=1, source_target_pairs={{0,2},{1,3},{2,0},{3,1},{4,6},{5,7},{6,4},{7,5},{8,10},{9,11},{10,... | collective-permute-start | bytes 196616 | tf_op jit(solution)/shard_map/ppermute | solution.py:205
  33.1 8.6 %collective-permute-start.11 = (bf16[2,16,1024]{2,1,0:T(8,128)(2,1)S(1)}, bf16[2,16,1024]{2,1,0:T(8,128)(2,1)S(1)}, u32[]{:S(2)}, u32[]{:S(2)}) collective-permute-start(bf16[2,16,1024]{2,1,0:T(8,128)(2,1)S(1)} %get-tuple-element.30), channel_id=1, source_target_pairs={{0,3},{1,2},{2,1},{3,0},{4,7},{5,6},{6,5},{7,4},{8,11},{9,10},{10,... | collective-permute-start | bytes 196616 | tf_op jit(solution)/shard_map/ppermute | solution.py:205
  37.2 4.6 %collective-permute-start.13 = (bf16[2,16,1024]{2,1,0:T(8,128)(2,1)S(1)}, bf16[2,16,1024]{2,1,0:T(8,128)(2,1)S(1)}, u32[]{:S(2)}, u32[]{:S(2)}) collective-permute-start(bf16[2,16,1024]{2,1,0:T(8,128)(2,1)S(1)} %get-tuple-element.34), channel_id=1, source_target_pairs={{0,1},{1,0},{2,3},{3,2},{4,5},{5,4},{6,7},{7,6},{8,9},{9,8},{10,11... | collective-permute-start | bytes 196616 | tf_op jit(solution)/shard_map/ppermute | solution.py:205
  37.3 6.0 %collective-permute-start.14 = (bf16[2,16,1024]{2,1,0:T(8,128)(2,1)S(1)}, bf16[2,16,1024]{2,1,0:T(8,128)(2,1)S(1)}, u32[]{:S(2)}, u32[]{:S(2)}) collective-permute-start(bf16[2,16,1024]{2,1,0:T(8,128)(2,1)S(1)} %get-tuple-element.35), channel_id=1, source_target_pairs={{0,2},{1,3},{2,0},{3,1},{4,6},{5,7},{6,4},{7,5},{8,10},{9,11},{10,... | collective-permute-start | bytes 196616 | tf_op jit(solution)/shard_map/ppermute | solution.py:205
  40.8 6.1 %collective-permute-start.15 = (bf16[2,16,1024]{2,1,0:T(8,128)(2,1)S(1)}, bf16[2,16,1024]{2,1,0:T(8,128)(2,1)S(1)}, u32[]{:S(2)}, u32[]{:S(2)}) collective-permute-start(bf16[2,16,1024]{2,1,0:T(8,128)(2,1)S(1)} %get-tuple-element.36), channel_id=1, source_target_pairs={{0,3},{1,2},{2,1},{3,0},{4,7},{5,6},{6,5},{7,4},{8,11},{9,10},{10,... | collective-permute-start | bytes 196616 | tf_op jit(solution)/shard_map/ppermute | solution.py:205

commit v4 on v3

--- a/solution.py
+++ b/solution.py
@@ -13,10 +13,6 @@
 VMEM_LIMIT = 40 * 1024 * 1024
 
 
-def normalized(ref):
-    return ref[...] / jnp.sum(ref[...], axis=1, keepdims=True)
-
-
 def select_taps(index, kernel):
     total = jnp.zeros((kernel.shape[0],) + index.shape[1:], F32)
     for tap in range(kernel.shape[1]):
@@ -29,11 +25,11 @@
     return pltpu.roll(spread, 0, 1, stride=1, stride_axis=0)
 
 
-def matrices_kernel(planes, strip, device_ref, kx_ref, ky_ref, kz_ref, w_ref, wt_ref, tf_ref, tb_ref):
-    views, taps = kx_ref.shape
+def matrices_kernel(planes, strip, device_ref, kernels_ref, w_ref, wt_ref, tf_ref, tb_ref):
+    views, taps = kernels_ref.shape[1:]
     margin = taps // 2
     extent = strip + 2 * HALO
-    kx, ky, kz = normalized(kx_ref), normalized(ky_ref), normalized(kz_ref)
+    kx, ky, kz = [kernels_ref[n] / jnp.sum(kernels_ref[n], axis=1, keepdims=True) for n in range(3)]
     lane = lax.broadcasted_iota(jnp.int32, (1, LANES), 1)
     x_row = select_taps(lane % extent - (HALO - margin), kx)
     near = jnp.where(lane < LANES // 2, lane, lane - LANES)
@@ -92,7 +88,7 @@
     return base + values[..., first : first + LANES].astype(F32)
 
 
-def main_kernel(planes, view_rows, place_ref, offsets_ref, *refs):
+def main_kernel(planes, view_rows, place_ref, device_ref, offsets_ref, *refs):
     quarters, (views_ref, w_ref, wt_ref, tf_ref, tb_ref) = refs[:4], refs[4:9]
     cores, backs, (ext_ref, pad_ref, back_ref, deep_ref) = refs[9:11], refs[11:13], refs[13:]
     views = offsets_ref.shape[0]
@@ -104,6 +100,12 @@
     for p in range(count):
         for n, ref in enumerate(quarters[::-1]):
             ext_ref[p * extent + n * HALO : p * extent + (n + 1) * HALO, :] = ref[p]
+
+    @pl.when(device_ref[2] == 0)
+    def _():
+        for p in range(count):
+            ext_ref[(p + 1) * extent - HALO : (p + 1) * extent, :] = jnp.zeros((HALO, columns), BF16)
+
     for pad in (pad_ref, back_ref):
         pad[:, :LANES] = jnp.zeros((pad.shape[0], LANES), BF16)
         pad[:, LANES + columns :] = jnp.zeros((pad.shape[0], LANES), BF16)
@@ -137,13 +139,14 @@
         write_coded(backs[1], (p, slice(None)), part[3 * HALO :])
 
 
-def join_kernel(planes, core_ref, other_ref, own_ref, *sends):
+def join_kernel(planes, flag, device_ref, core_ref, other_ref, own_ref, *sends):
     columns = core_ref.shape[2]
+    counts = device_ref[flag] != 0
     for p in range(core_ref.shape[0]):
         other = other_ref[p]
         parts = []
         for first in range(0, columns, LANES):
-            parts.append(core_ref[p, :, first : first + LANES] + decoded(other, first))
+            parts.append(core_ref[p, :, first : first + LANES] + jnp.where(counts, decoded(other, first), 0.0))
         whole = jnp.concatenate(parts, axis=1)
         if p < planes:
             own_ref[p] = whole
@@ -198,14 +201,16 @@
     tile = lax.axis_index("tile").astype(jnp.int32)
     odd = tile % 2
     place = (tile * strip).reshape(1)
-    device = jnp.stack([lax.axis_index("depth").astype(jnp.int32), odd])
+    has_chip = ((tile > 0) & (tile < tiles - 1)).astype(jnp.int32)
+    block_index = lax.axis_index("depth").astype(jnp.int32)
+    device = jnp.stack([block_index, odd, has_chip, jnp.ones_like(odd)])
     assert strip == 2 * HALO and tiles % 2 == 0
 
     def across(array, step):
         return lax.ppermute(array, "depth", [(i, i ^ step) for i in range(depth)])
 
     def beside(array):
-        return lax.ppermute(array, "tile", [(i, i - 1 + 2 * (i % 2)) for i in range(1, tiles - 1)])
+        return lax.ppermute(array, "tile", [(i, (i - 1 + 2 * (i % 2)) % tiles) for i in range(tiles)])
 
     def within(array):
         return lax.ppermute(array, "tile", [(i, i ^ 1) for i in range(tiles)])
@@ -221,13 +226,13 @@
         functools.partial(matrices_kernel, planes, strip),
         (shape((rows, span), BF16), shape((span, rows), BF16))
         + (shape((count, WIDE + 2 * LANES, WIDE), BF16),) * 2,
-        1, 3, flops=10**8, moved=5 * 2**20,
-    )(device, kernel_x, kernel_y, kernel_z)
+        1, 1, flops=10**8, moved=5 * 2**20,
+    )(device, jnp.stack([kernel_x, kernel_y, kernel_z]))
     halves = (depth * planes, HALO, columns)
     inner, outer, to_core, to_chip = call(
         functools.partial(main_kernel, planes, view_rows),
         (shape(halves, F32),) * 2 + (shape(halves, BF16),) * 2,
-        2, 9,
+        3, 9,
         scratch=(
             pltpu.VMEM((span, columns), BF16),
             pltpu.VMEM((rows, columns + 2 * LANES), BF16),
@@ -235,15 +240,15 @@
             pltpu.VMEM((rows, columns), BF16),
         ),
         flops=2 * 10**9, moved=10 * 2**20,
-    )(place, offsets, other_chip, outer, inner, other_core, views.reshape(rows, columns), w, wt, tf, tb)
+    )(place, device, offsets, other_chip, outer, inner, other_core, views.reshape(rows, columns), w, wt, tf, tb)
     block = (planes, HALO, columns)
     sums = []
-    for core, other in ((inner, within(to_core)), (outer, beside(to_chip))):
+    for flag, core, other in ((3, inner, within(to_core)), (2, outer, beside(to_chip))):
         own_sum, *sends = call(
-            functools.partial(join_kernel, planes),
+            functools.partial(join_kernel, planes, flag),
             (shape(block, F32),) + (shape(block, BF16),) * (depth - 1),
-            0, 2, flops=10**6, moved=3 * 2**20,
-        )(core, other)
+            1, 2, flops=10**6, moved=3 * 2**20,
+        )(device, core, other)
         sums += [own_sum] + [across(send, step + 1) for step, send in enumerate(sends)]
     return call(
         functools.partial(update_kernel, view_rows),

time: 48.5 us -> 49.3 us (1.016)
  the two profiles are of different devices: /device:TPU:4 before, /device:TPU:0 now
where the time goes in v4:
time: 49.3 us; the launch traced here: 49.1 us
  starting transfers between devices  20.3 us (41%)
  waiting for transfers between devices  18.1 us (37%)
  Pallas kernels  8.53 us (17%)
  other arithmetic  1.94 us (4%)
    ppermute x12, starting transfers between devices, across(): return lax.ppermute(array, 'depth', [(i, i ^ step) for i in range(depth)])  19.2 us
    ppermute x12, waiting for transfers between devices, across(): return lax.ppermute(array, 'depth', [(i, i ^ step) for i in range(depth)])  10.8 us
    ppermute x2, waiting for transfers between devices, beside(): lax.ppermute(array, 'tile', [(i, (i - 1 + 2 * (i % 2)) % tiles) for i in...  6.49 us
    pallas_call x1, Pallas kernels, shards(): call(functools.partial(main_kernel, planes, view_rows), (shape(halves, F3...  3.99 us
    pallas_call x1, Pallas kernels, shards(): call(functools.partial(matrices_kernel, planes, strip), (shape((rows, spa...  1.88 us
    pallas_call x1, Pallas kernels, shards(): call(functools.partial(update_kernel, view_rows), shape(estimate.shape, F...  1.38 us
    pallas_call x2, Pallas kernels, shards(): call(functools.partial(join_kernel, planes, flag), (shape(block, F32),) +...  1.28 us
    convert_element_type x1, other arithmetic, shards(): own = estimate.astype(BF16)  1.05 us
  transfers between devices with their start and end apart: 16, of which 8 were waited for; matrix products, arithmetic and copies ran while one was open for 2% of the time, Pallas kernels for 6%

profile of v4, /device:TPU:0, one launch (start us, length us, event | category | flops | bytes accessed | tf_op | source)
XLA Modules:
  0.0 49.1 jit_solution(18081786302749544890)
XLA Ops:
  0.0 0.0 copy-start.1
  0.0 0.0 copy-start.2
  0.0 1.1 %convert_element_type.4 = bf16[2,32,1024]{2,1,0:T(8,128)(2,1)S(1)} convert(f32[2,32,1024]{2,1,0:T(8,128)} %estimate_ref.1) | non-fusion elementwise | flops 65536 | bytes 393216 | tf_op jit(solution)/shard_map/convert_element_type | solution.py:218
  1.1 5.1 %collective-permute-start.2 = (bf16[2,16,1024]{2,1,0:T(8,128)(2,1)S(1)}, bf16[2,16,1024]{2,1,0:T(8,128)(2,1)S(1)}, u32[]{:S(2)}, u32[]{:S(2)}) collective-permute-start(bf16[2,16,1024]{2,1,0:T(8,128)(2,1)S(1)} %get-tuple-element.38), channel_id=1, source_target_pairs={{0,3},{1,2},{2,1},{3,0},{4,7},{5,6},{6,5},{7,4},{8,11},{9,10},{10,... | collective-permute-start | bytes 196616 | tf_op jit(solution)/shard_map/ppermute | solution.py:210
  6.2 0.0 collective-permute-start.1
  6.2 0.6 %collective-permute-start = (bf16[2,16,1024]{2,1,0:T(8,128)(2,1)S(1)}, bf16[2,16,1024]{2,1,0:T(8,128)(2,1)S(1)}, u32[]{:S(2)}, u32[]{:S(2)}) collective-permute-start(bf16[2,16,1024]{2,1,0:T(8,128)(2,1)S(1)} %get-tuple-element.38), channel_id=1, source_target_pairs={{0,1},{1,0},{2,3},{3,2},{4,5},{5,4},{6,7},{7,6},{8,9},{9,8},{10,11... | collective-permute-start | bytes 196616 | tf_op jit(solution)/shard_map/ppermute | solution.py:210
  6.8 3.7 %collective-permute-start.6 = (bf16[2,16,1024]{2,1,0:T(8,128)(2,1)S(1)}, bf16[2,16,1024]{2,1,0:T(8,128)(2,1)S(1)}, u32[]{:S(2)}, u32[]{:S(2)}) collective-permute-start(bf16[2,16,1024]{2,1,0:T(8,128)(2,1)S(1)} %get-tuple-element.37), channel_id=1, source_target_pairs={{0,3},{1,2},{2,1},{3,0},{4,7},{5,6},{6,5},{7,4},{8,11},{9,10},{10,... | collective-permute-start | bytes 196616 | tf_op jit(solution)/shard_map/ppermute | solution.py:210
  10.6 0.0 collective-permute-start.5
  10.6 0.0 collective-permute-done.2
  10.6 0.8 %collective-permute-start.4 = (bf16[2,16,1024]{2,1,0:T(8,128)(2,1)S(1)}, bf16[2,16,1024]{2,1,0:T(8,128)(2,1)S(1)}, u32[]{:S(2)}, u32[]{:S(2)}) collective-permute-start(bf16[2,16,1024]{2,1,0:T(8,128)(2,1)S(1)} %get-tuple-element.37), channel_id=1, source_target_pairs={{0,1},{1,0},{2,3},{3,2},{4,5},{5,4},{6,7},{7,6},{8,9},{9,8},{10,11... | collective-permute-start | bytes 196616 | tf_op jit(solution)/shard_map/ppermute | solution.py:210
  11.4 3.4 %collective-permute-done.1 = bf16[2,16,1024]{2,1,0:T(8,128)(2,1)S(1)} collective-permute-done((bf16[2,16,1024]{2,1,0:T(8,128)(2,1)S(1)}, bf16[2,16,1024]{2,1,0:T(8,128)(2,1)S(1)}, u32[]{:S(2)}, u32[]{:S(2)}) %collective-permute-start.1) | collective-permute-done | bytes 65568 | tf_op jit(solution)/shard_map/ppermute | solution.py:210
  14.8 0.0 collective-permute-done
  14.8 0.4 collective-permute-start.3
  15.2 0.0 collective-permute-done.6
  15.2 2.2 %collective-permute-done.5 = bf16[2,16,1024]{2,1,0:T(8,128)(2,1)S(1)} collective-permute-done((bf16[2,16,1024]{2,1,0:T(8,128)(2,1)S(1)}, bf16[2,16,1024]{2,1,0:T(8,128)(2,1)S(1)}, u32[]{:S(2)}, u32[]{:S(2)}) %collective-permute-start.5) | collective-permute-done | bytes 65568 | tf_op jit(solution)/shard_map/ppermute | solution.py:210
  17.4 0.0 collective-permute-done.4
  17.5 0.1 collective-permute-start.7
  17.6 0.1 pad_add_fusion.device_ref
  17.6 0.7 %pad_maximum_fusion.2.kernels_ref = f32[3,8,31]{2,1,0:T(8,128)S(1)} fusion(f32[1,8,31]{2,1,0:T(8,128)} %bitcast.9, f32[1,8,31]{2,1,0:T(8,128)} %bitcast.10, f32[1,8,31]{2,1,0:T(8,128)} %bitcast.11), kind=kLoop, calls=%fused_computation.4 | loop fusion | flops 1488 | bytes 5952 | tf_op jit(solution)/shard_map/stack | solution.py:230
  18.4 1.9 %shard_map.64 = (bf16[512,512]{1,0:T(8,128)(2,1)S(1)}, bf16[512,512]{1,0:T(8,128)(2,1)S(1)}, bf16[8,512,256]{2,1,0:T(8,128)(2,1)S(1)}, bf16[8,512,256]{2,1,0:T(8,128)(2,1)S(1)}) custom-call(s32[4]{0:T(128)S(1)} %pad_add_fusion.device_ref, f32[3,8,31]{2,1,0:T(8,128)S(1)} %pad_maximum_fusion.2.kernels_ref), custom_call_target="tpu_custom_call" | custom-call | flops 100000000 | bytes 5242880 | tf_op jit(solution)/shard_map/pallas_call | solution.py:225
  20.2 3.9 %collective-permute-done.3.refs_0_ = bf16[8,16,1024]{2,1,0:T(8,128)(2,1)S(1)} collective-permute-done((bf16[8,16,1024]{2,1,0:T(8,128)(2,1)S(1)}, bf16[8,16,1024]{2,1,0:T(8,128)(2,1)S(1)}, u32[]{:S(2)}, u32[]{:S(2)}) %collective-permute-start.3) | collective-permute-done | bytes 262176 | tf_op jit(solution)/shard_map/ppermute | solution.py:213
  24.1 0.0 collective-permute-done.7.refs_3_
  24.1 0.0 copy-done.1
  24.1 0.0 copy-done.2
  24.2 0.0 copy-start
  24.2 4.0 %shard_map.65 = (f32[8,16,1024]{2,1,0:T(8,128)S(1)}, f32[8,16,1024]{2,1,0:T(8,128)S(1)}, bf16[8,16,1024]{2,1,0:T(8,128)(2,1)S(1)}, bf16[8,16,1024]{2,1,0:T(8,128)(2,1)S(1)}) custom-call(s32[1]{0:T(128)} %bitcast.place_ref, s32[4]{0:T(128)S(1)} %pad_add_fusion.device_ref, s32[8]{0:T(128)S(1)} %copy-done.1, ...), custom_call_target="tpu_custom_call" | custom-call | flops 2000000000 | bytes 10485760 | tf_op jit(solution)/shard_map/pallas_call | solution.py:232
  28.2 0.1 collective-permute-start.8
  28.2 0.6 %collective-permute-start.12 = (bf16[8,16,1024]{2,1,0:T(8,128)(2,1)S(1)}, bf16[8,16,1024]{2,1,0:T(8,128)(2,1)S(1)}, u32[]{:S(2)}, u32[]{:S(2)}) collective-permute-start(bf16[8,16,1024]{2,1,0:T(8,128)(2,1)S(1)} %get-tuple-element.32), channel_id=1, source_target_pairs={{0,28},{4,8},{8,4},{12,16},{16,12},{20,24},{24,20},{28,0},{1,29},{... | collective-permute-start | bytes 786440 | tf_op jit(solution)/shard_map/ppermute | solution.py:213
  28.9 0.9 %collective-permute-done.8.other_ref = bf16[8,16,1024]{2,1,0:T(8,128)(2,1)S(1)} collective-permute-done((bf16[8,16,1024]{2,1,0:T(8,128)(2,1)S(1)}, bf16[8,16,1024]{2,1,0:T(8,128)(2,1)S(1)}, u32[]{:S(2)}, u32[]{:S(2)}) %collective-permute-start.8) | collective-permute-done | bytes 262176 | tf_op jit(solution)/shard_map/ppermute | solution.py:216
  29.8 0.6 %shard_map.66 = (f32[2,16,1024]{2,1,0:T(8,128)S(1)}, bf16[2,16,1024]{2,1,0:T(8,128)(2,1)S(1)}, bf16[2,16,1024]{2,1,0:T(8,128)(2,1)S(1)}, bf16[2,16,1024]{2,1,0:T(8,128)(2,1)S(1)}) custom-call(s32[4]{0:T(128)S(1)} %pad_add_fusion.device_ref, f32[8,16,1024]{2,1,0:T(8,128)S(1)} %get-tuple-element.25.core_ref, ...), custom_call_target="tpu_custom_call" | custom-call | flops 1000000 | bytes 3145728 | tf_op jit(solution)/shard_map/pallas_call | solution.py:247
  30.4 0.1 collective-permute-start.9
  30.5 3.3 %collective-permute-start.10 = (bf16[2,16,1024]{2,1,0:T(8,128)(2,1)S(1)}, bf16[2,16,1024]{2,1,0:T(8,128)(2,1)S(1)}, u32[]{:S(2)}, u32[]{:S(2)}) collective-permute-start(bf16[2,16,1024]{2,1,0:T(8,128)(2,1)S(1)} %get-tuple-element.29), channel_id=1, source_target_pairs={{0,2},{1,3},{2,0},{3,1},{4,6},{5,7},{6,4},{7,5},{8,10},{9,11},{10,... | collective-permute-start | bytes 196616 | tf_op jit(solution)/shard_map/ppermute | solution.py:210
  33.7 1.1 %collective-permute-start.11 = (bf16[2,16,1024]{2,1,0:T(8,128)(2,1)S(1)}, bf16[2,16,1024]{2,1,0:T(8,128)(2,1)S(1)}, u32[]{:S(2)}, u32[]{:S(2)}) collective-permute-start(bf16[2,16,1024]{2,1,0:T(8,128)(2,1)S(1)} %get-tuple-element.30), channel_id=1, source_target_pairs={{0,3},{1,2},{2,1},{3,0},{4,7},{5,6},{6,5},{7,4},{8,11},{9,10},{10,... | collective-permute-start | bytes 196616 | tf_op jit(solution)/shard_map/ppermute | solution.py:210
  34.9 2.6 %collective-permute-done.12.other_ref = bf16[8,16,1024]{2,1,0:T(8,128)(2,1)S(1)} collective-permute-done((bf16[8,16,1024]{2,1,0:T(8,128)(2,1)S(1)}, bf16[8,16,1024]{2,1,0:T(8,128)(2,1)S(1)}, u32[]{:S(2)}, u32[]{:S(2)}) %collective-permute-start.12) | collective-permute-done | bytes 262176 | tf_op jit(solution)/shard_map/ppermute | solution.py:213
  37.5 0.6 %shard_map.67 = (f32[2,16,1024]{2,1,0:T(8,128)S(1)}, bf16[2,16,1024]{2,1,0:T(8,128)(2,1)S(1)}, bf16[2,16,1024]{2,1,0:T(8,128)(2,1)S(1)}, bf16[2,16,1024]{2,1,0:T(8,128)(2,1)S(1)}) custom-call(s32[4]{0:T(128)S(1)} %pad_add_fusion.device_ref, f32[8,16,1024]{2,1,0:T(8,128)S(1)} %get-tuple-element.31.core_ref, ...), custom_call_target="tpu_custom_call" | custom-call | flops 1000000 | bytes 3145728 | tf_op jit(solution)/shard_map/pallas_call | solution.py:247
  38.1 0.1 collective-permute-start.13
  38.2 3.5 %collective-permute-start.14 = (bf16[2,16,1024]{2,1,0:T(8,128)(2,1)S(1)}, bf16[2,16,1024]{2,1,0:T(8,128)(2,1)S(1)}, u32[]{:S(2)}, u32[]{:S(2)}) collective-permute-start(bf16[2,16,1024]{2,1,0:T(8,128)(2,1)S(1)} %get-tuple-element.35), channel_id=1, source_target_pairs={{0,2},{1,3},{2,0},{3,1},{4,6},{5,7},{6,4},{7,5},{8,10},{9,11},{10,... | collective-permute-start | bytes 196616 | tf_op jit(solution)/shard_map/ppermute | solution.py:210
  41.6 0.0 collective-permute-done.9.refs_1_
  41.6 0.9 %collective-permute-start.15 = (bf16[2,16,1024]{2,1,0:T(8,128)(2,1)S(1)}, bf16[2,16,1024]{2,1,0:T(8,128)(2,1)S(1)}, u32[]{:S(2)}, u32[]{:S(2)}) collective-permute-start(bf16[2,16,1024]{2,1,0:T(8,128)(2,1)S(1)} %get-tuple-element.36), channel_id=1, source_target_pairs={{0,3},{1,2},{2,1},{3,0},{4,7},{5,6},{6,5},{7,4},{8,11},{9,10},{10,... | collective-permute-start | bytes 196616 | tf_op jit(solution)/shard_map/ppermute | solution.py:210
  42.5 0.0 collective-permute-done.10.refs_2_
  42.6 0.0 collective-permute-done.11.refs_3_
  42.6 0.6 %collective-permute-done.13.refs_5_ = bf16[2,16,1024]{2,1,0:T(8,128)(2,1)S(1)} collective-permute-done((bf16[2,16,1024]{2,1,0:T(8,128)(2,1)S(1)}, bf16[2,16,1024]{2,1,0:T(8,128)(2,1)S(1)}, u32[]{:S(2)}, u32[]{:S(2)}) %collective-permute-start.13) | collective-permute-done | bytes 65568 | tf_op jit(solution)/shard_map/ppermute | solution.py:210
  43.1 2.9 %collective-permute-done.14.refs_6_ = bf16[2,16,1024]{2,1,0:T(8,128)(2,1)S(1)} collective-permute-done((bf16[2,16,1024]{2,1,0:T(8,128)(2,1)S(1)}, bf16[2,16,1024]{2,1,0:T(8,128)(2,1)S(1)}, u32[]{:S(2)}, u32[]{:S(2)}) %collective-permute-start.14) | collective-permute-done | bytes 65568 | tf_op jit(solution)/shard_map/ppermute | solution.py:210
  46.0 1.7 %collective-permute-done.15.refs_7_ = bf16[2,16,1024]{2,1,0:T(8,128)(2,1)S(1)} collective-permute-done((bf16[2,16,1024]{2,1,0:T(8,128)(2,1)S(1)}, bf16[2,16,1024]{2,1,0:T(8,128)(2,1)S(1)}, u32[]{:S(2)}, u32[]{:S(2)}) %collective-permute-start.15) | collective-permute-done | bytes 65568 | tf_op jit(solution)/shard_map/ppermute | solution.py:210
  47.7 0.0 copy-done
  47.7 1.4 %shard_map.68 = f32[2,32,1024]{2,1,0:T(8,128)} custom-call(s32[1]{0:T(128)} %bitcast.place_ref, s32[4]{0:T(128)S(1)} %pad_add_fusion.device_ref, s32[8]{0:T(128)S(1)} %copy-done.1, f32[2,32,1024]{2,1,0:T(8,128)S(1)} %copy-done, f32[2,16,1024]{2,1,0:T(8,128)S(1)} %get-tuple-element.27.refs_0_, bf16[2,16,1024]{2,1,0:T(8,128)(2,1)S(1)} %collective-permute-done.9.refs_1_, ...), custom_call_target="tpu_custom_call" | custom-call | flops 1000000 | bytes 1048576 | tf_op jit(solution)/shard_map/pallas_call | solution.py:253
  (3 shorter events, 0.1 us)
Async XLA Ops:
  0.0 24.1 %copy-start.1 = (s32[8]{0:T(128)S(1)}, s32[8]{0:T(128)}, u32[]{:S(2)}) copy-start(s32[8]{0:T(128)} %offsets_ref.3) | copy-start | bytes 100
  0.0 24.1 %copy-start.2 = (bf16[8,2,32,1024]{3,2,1,0:T(8,128)(2,1)S(1)}, bf16[8,2,32,1024]{3,2,1,0:T(8,128)(2,1)}, u32[]{:S(2)}) copy-start(bf16[8,2,32,1024]{3,2,1,0:T(8,128)(2,1)} %param.7) | copy-start | bytes 3145732
  1.1 9.5 %collective-permute-start.2 = (bf16[2,16,1024]{2,1,0:T(8,128)(2,1)S(1)}, bf16[2,16,1024]{2,1,0:T(8,128)(2,1)S(1)}, u32[]{:S(2)}, u32[]{:S(2)}) collective-permute-start(bf16[2,16,1024]{2,1,0:T(8,128)(2,1)S(1)} %get-tuple-element.38), channel_id=1, source_target_pairs={{0,3},{1,2},{2,1},{3,0},{4,7},{5,6},{6,5},{7,4},{8,11},{9,10},{10,... | collective-permute-start | bytes 196616 | tf_op jit(solution)/shard_map/ppermute | solution.py:210
  6.2 8.6 %collective-permute-start.1 = (bf16[2,16,1024]{2,1,0:T(8,128)(2,1)S(1)}, bf16[2,16,1024]{2,1,0:T(8,128)(2,1)S(1)}, u32[]{:S(2)}, u32[]{:S(2)}) collective-permute-start(bf16[2,16,1024]{2,1,0:T(8,128)(2,1)S(1)} %get-tuple-element.38), channel_id=1, source_target_pairs={{0,2},{1,3},{2,0},{3,1},{4,6},{5,7},{6,4},{7,5},{8,10},{9,11},{10,... | collective-permute-start | bytes 196616 | tf_op jit(solution)/shard_map/ppermute | solution.py:210
  6.2 8.6 %collective-permute-start = (bf16[2,16,1024]{2,1,0:T(8,128)(2,1)S(1)}, bf16[2,16,1024]{2,1,0:T(8,128)(2,1)S(1)}, u32[]{:S(2)}, u32[]{:S(2)}) collective-permute-start(bf16[2,16,1024]{2,1,0:T(8,128)(2,1)S(1)} %get-tuple-element.38), channel_id=1, source_target_pairs={{0,1},{1,0},{2,3},{3,2},{4,5},{5,4},{6,7},{7,6},{8,9},{9,8},{10,11... | collective-permute-start | bytes 196616 | tf_op jit(solution)/shard_map/ppermute | solution.py:210
  6.8 8.4 %collective-permute-start.6 = (bf16[2,16,1024]{2,1,0:T(8,128)(2,1)S(1)}, bf16[2,16,1024]{2,1,0:T(8,128)(2,1)S(1)}, u32[]{:S(2)}, u32[]{:S(2)}) collective-permute-start(bf16[2,16,1024]{2,1,0:T(8,128)(2,1)S(1)} %get-tuple-element.37), channel_id=1, source_target_pairs={{0,3},{1,2},{2,1},{3,0},{4,7},{5,6},{6,5},{7,4},{8,11},{9,10},{10,... | collective-permute-start | bytes 196616 | tf_op jit(solution)/shard_map/ppermute | solution.py:210
  10.6 6.8 %collective-permute-start.5 = (bf16[2,16,1024]{2,1,0:T(8,128)(2,1)S(1)}, bf16[2,16,1024]{2,1,0:T(8,128)(2,1)S(1)}, u32[]{:S(2)}, u32[]{:S(2)}) collective-permute-start(bf16[2,16,1024]{2,1,0:T(8,128)(2,1)S(1)} %get-tuple-element.37), channel_id=1, source_target_pairs={{0,2},{1,3},{2,0},{3,1},{4,6},{5,7},{6,4},{7,5},{8,10},{9,11},{10,... | collective-permute-start | bytes 196616 | tf_op jit(solution)/shard_map/ppermute | solution.py:210
  10.6 6.8 %collective-permute-start.4 = (bf16[2,16,1024]{2,1,0:T(8,128)(2,1)S(1)}, bf16[2,16,1024]{2,1,0:T(8,128)(2,1)S(1)}, u32[]{:S(2)}, u32[]{:S(2)}) collective-permute-start(bf16[2,16,1024]{2,1,0:T(8,128)(2,1)S(1)} %get-tuple-element.37), channel_id=1, source_target_pairs={{0,1},{1,0},{2,3},{3,2},{4,5},{5,4},{6,7},{7,6},{8,9},{9,8},{10,11... | collective-permute-start | bytes 196616 | tf_op jit(solution)/shard_map/ppermute | solution.py:210
  14.8 9.3 %collective-permute-start.3 = (bf16[8,16,1024]{2,1,0:T(8,128)(2,1)S(1)}, bf16[8,16,1024]{2,1,0:T(8,128)(2,1)S(1)}, u32[]{:S(2)}, u32[]{:S(2)}) collective-permute-start(bf16[8,16,1024]{2,1,0:T(8,128)(2,1)S(1)} %pad_maximum_fusion.refs_1_), channel_id=1, source_target_pairs={{0,28},{4,8},{8,4},{12,16},{16,12},{20,24},{24,20},{28,0},{1,29},{... | collective-permute-start | bytes 786440 | tf_op jit(solution)/shard_map/ppermute | solution.py:213
  17.5 6.7 %collective-permute-start.7 = (bf16[8,16,1024]{2,1,0:T(8,128)(2,1)S(1)}, bf16[8,16,1024]{2,1,0:T(8,128)(2,1)S(1)}, u32[]{:S(2)}, u32[]{:S(2)}) collective-permute-start(bf16[8,16,1024]{2,1,0:T(8,128)(2,1)S(1)} %pad_maximum_fusion.1.refs_2_), channel_id=1, source_target_pairs={{0,4},{4,0},{8,12},{12,8},{16,20},{20,16},{24,28},{28,24},{1,5},{5... | collective-permute-start | bytes 786440 | tf_op jit(solution)/shard_map/ppermute | solution.py:216
  24.2 23.5 %copy-start = (f32[2,32,1024]{2,1,0:T(8,128)S(1)}, f32[2,32,1024]{2,1,0:T(8,128)}, u32[]{:S(2)}) copy-start(f32[2,32,1024]{2,1,0:T(8,128)} %estimate_ref.1) | copy-start | bytes 786436
  28.2 1.6 %collective-permute-start.8 = (bf16[8,16,1024]{2,1,0:T(8,128)(2,1)S(1)}, bf16[8,16,1024]{2,1,0:T(8,128)(2,1)S(1)}, u32[]{:S(2)}, u32[]{:S(2)}) collective-permute-start(bf16[8,16,1024]{2,1,0:T(8,128)(2,1)S(1)} %get-tuple-element.26), channel_id=1, source_target_pairs={{0,4},{4,0},{8,12},{12,8},{16,20},{20,16},{24,28},{28,24},{1,5},{5... | collective-permute-start | bytes 786440 | tf_op jit(solution)/shard_map/ppermute | solution.py:216
  28.2 9.2 %collective-permute-start.12 = (bf16[8,16,1024]{2,1,0:T(8,128)(2,1)S(1)}, bf16[8,16,1024]{2,1,0:T(8,128)(2,1)S(1)}, u32[]{:S(2)}, u32[]{:S(2)}) collective-permute-start(bf16[8,16,1024]{2,1,0:T(8,128)(2,1)S(1)} %get-tuple-element.32), channel_id=1, source_target_pairs={{0,28},{4,8},{8,4},{12,16},{16,12},{20,24},{24,20},{28,0},{1,29},{... | collective-permute-start | bytes 786440 | tf_op jit(solution)/shard_map/ppermute | solution.py:213
  30.4 11.2 %collective-permute-start.9 = (bf16[2,16,1024]{2,1,0:T(8,128)(2,1)S(1)}, bf16[2,16,1024]{2,1,0:T(8,128)(2,1)S(1)}, u32[]{:S(2)}, u32[]{:S(2)}) collective-permute-start(bf16[2,16,1024]{2,1,0:T(8,128)(2,1)S(1)} %get-tuple-element.28), channel_id=1, source_target_pairs={{0,1},{1,0},{2,3},{3,2},{4,5},{5,4},{6,7},{7,6},{8,9},{9,8},{10,11... | collective-permute-start | bytes 196616 | tf_op jit(solution)/shard_map/ppermute | solution.py:210
  30.5 12.1 %collective-permute-start.10 = (bf16[2,16,1024]{2,1,0:T(8,128)(2,1)S(1)}, bf16[2,16,1024]{2,1,0:T(8,128)(2,1)S(1)}, u32[]{:S(2)}, u32[]{:S(2)}) collective-permute-start(bf16[2,16,1024]{2,1,0:T(8,128)(2,1)S(1)} %get-tuple-element.29), channel_id=1, source_target_pairs={{0,2},{1,3},{2,0},{3,1},{4,6},{5,7},{6,4},{7,5},{8,10},{9,11},{10,... | collective-permute-start | bytes 196616 | tf_op jit(solution)/shard_map/ppermute | solution.py:210
  33.7 8.8 %collective-permute-start.11 = (bf16[2,16,1024]{2,1,0:T(8,128)(2,1)S(1)}, bf16[2,16,1024]{2,1,0:T(8,128)(2,1)S(1)}, u32[]{:S(2)}, u32[]{:S(2)}) collective-permute-start(bf16[2,16,1024]{2,1,0:T(8,128)(2,1)S(1)} %get-tuple-element.30), channel_id=1, source_target_pairs={{0,3},{1,2},{2,1},{3,0},{4,7},{5,6},{6,5},{7,4},{8,11},{9,10},{10,... | collective-permute-start | bytes 196616 | tf_op jit(solution)/shard_map/ppermute | solution.py:210
  38.1 5.0 %collective-permute-start.13 = (bf16[2,16,1024]{2,1,0:T(8,128)(2,1)S(1)}, bf16[2,16,1024]{2,1,0:T(8,128)(2,1)S(1)}, u32[]{:S(2)}, u32[]{:S(2)}) collective-permute-start(bf16[2,16,1024]{2,1,0:T(8,128)(2,1)S(1)} %get-tuple-element.34), channel_id=1, source_target_pairs={{0,1},{1,0},{2,3},{3,2},{4,5},{5,4},{6,7},{7,6},{8,9},{9,8},{10,11... | collective-permute-start | bytes 196616 | tf_op jit(solution)/shard_map/ppermute | solution.py:210
  38.2 7.9 %collective-permute-start.14 = (bf16[2,16,1024]{2,1,0:T(8,128)(2,1)S(1)}, bf16[2,16,1024]{2,1,0:T(8,128)(2,1)S(1)}, u32[]{:S(2)}, u32[]{:S(2)}) collective-permute-start(bf16[2,16,1024]{2,1,0:T(8,128)(2,1)S(1)} %get-tuple-element.35), channel_id=1, source_target_pairs={{0,2},{1,3},{2,0},{3,1},{4,6},{5,7},{6,4},{7,5},{8,10},{9,11},{10,... | collective-permute-start | bytes 196616 | tf_op jit(solution)/shard_map/ppermute | solution.py:210
  41.6 6.1 %collective-permute-start.15 = (bf16[2,16,1024]{2,1,0:T(8,128)(2,1)S(1)}, bf16[2,16,1024]{2,1,0:T(8,128)(2,1)S(1)}, u32[]{:S(2)}, u32[]{:S(2)}) collective-permute-start(bf16[2,16,1024]{2,1,0:T(8,128)(2,1)S(1)} %get-tuple-element.36), channel_id=1, source_target_pairs={{0,3},{1,2},{2,1},{3,0},{4,7},{5,6},{6,5},{7,4},{8,11},{9,10},{10,... | collective-permute-start | bytes 196616 | tf_op jit(solution)/shard_map/ppermute | solution.py:210
